TPU v7x, 32 devices: a whole 2x2x4 slice. The times are simulated.
32 devices in a mesh: comp: 8 (over z, y), rank: 4 (over x, core).
Axes of the slice: x: 2, y: 2, z: 4, core: 2. Of those that a mesh axis runs over, the one named last changes fastest.
Arguments:
- density: float32 [32, 16384], P('comp'), may hold values from 0.1 to 1
- row_left: float32 [8, 32], replicated, may hold values from -4 to 4
- col_left: float32 [8, 16384], replicated, may hold values from -4 to 4
- row_right: float32 [8, 32], replicated, may hold values from -4 to 4
- col_right: float32 [8, 16384], replicated, may hold values from -4 to 4
Outputs:
- gain: float32 [32, 16384], P(('comp', 'rank'))
All inputs are finite; a program needn't handle non-finite values.
Results may differ from a plain program's by a relative error of at most 0.00021.
Values sent between devices are 32-bit elements; how exact they have to be, the bound alone decides.
No kernel may reach another device: no remote copies, remote signals or barrier semaphores. Data moves between devices by JAX's collectives and lax.ppermute only.
A program may use at most 192 MiB of HBM per device.

v0:
```python
import math

import jax
import jax.numpy as jnp
import numpy as np
from jax import lax
from jax.experimental import pallas as pl
from jax.experimental.pallas import tpu as pltpu
from jax.sharding import PartitionSpec as P

LANES = 128
VMEM_BYTES = 28 * 1024 * 1024
AXES = ("comp", "rank")
PAD = 4
HELD_PARTS = (0, 2, 1, 3)


def split_parts(values):
    high = values.astype(jnp.bfloat16)
    low = (values - high.astype(jnp.float32)).astype(jnp.bfloat16)
    return high, low


def split_rows(table):
    high, low = split_parts(jnp.asarray(table, jnp.float32))
    return jnp.concatenate([high, high, low], axis=0)


def split_columns(table):
    high, low = split_parts(jnp.asarray(table, jnp.float32))
    return jnp.concatenate([high, high, low], axis=1)


def dot_split(rows, table):
    high, low = split_parts(rows)
    joined = jnp.concatenate([high, low, high], axis=1)
    return jnp.dot(joined, table, preferred_element_type=jnp.float32)


def forward_table():
    angles = 2.0 * np.pi * np.outer(np.arange(LANES), np.arange(LANES)) / LANES
    cosine, sine = np.cos(angles), np.sin(angles)
    return np.block([[cosine, -sine], [sine, cosine]])


def inverse_table():
    angles = 2.0 * np.pi * np.outer(np.arange(LANES), np.arange(LANES)) / LANES
    return np.concatenate([np.cos(angles), -np.sin(angles)], axis=0)


def block_twiddles(blocks):
    angles = 2.0 * np.pi * np.outer(np.arange(blocks), np.arange(LANES)) / (blocks * LANES)
    table = np.stack([np.cos(angles), -np.sin(angles)], axis=1)
    return jnp.asarray(
        np.broadcast_to(table[:, :, None, :], (blocks, 2, 8, LANES)), jnp.float32
    )


def final_tables(devices, groups, blocks, width):
    owner = np.arange(devices) % groups
    frequency = (owner[:, None] + groups * np.arange(blocks)[None, :]).astype(np.float64) + 0.25
    frequency = np.broadcast_to(frequency[:, None, :], (devices, 2, blocks))
    inner = 2.0 * np.pi * frequency[..., None] * np.arange(LANES) / width
    rows = devices * 2 * blocks
    inner_cos = np.cos(inner).reshape(rows, LANES)
    inner_sin = np.sin(inner).reshape(rows, LANES)
    outer_count = width // LANES
    outer = 2.0 * np.pi * frequency * LANES / width
    outer = np.arange(outer_count)[:, None] * outer.reshape(1, rows)
    is_real = np.broadcast_to(np.array([True, False])[None, :, None], (devices, 2, blocks))
    is_real = is_real.reshape(1, rows)
    with_cos = np.where(is_real, np.cos(outer), -np.sin(outer))
    with_sin = np.where(is_real, -np.sin(outer), -np.cos(outer))
    return inner_cos, inner_sin, np.concatenate([with_cos, with_sin], axis=1)


def block_fourier(reals, imags):
    count = len(reals)
    if count == 1:
        return reals, imags
    if count == 2:
        return (
            [reals[0] + reals[1], reals[0] - reals[1]],
            [imags[0] + imags[1], imags[0] - imags[1]],
        )
    even_real, odd_real = reals[0] + reals[2], reals[0] - reals[2]
    even_imag, odd_imag = imags[0] + imags[2], imags[0] - imags[2]
    pair_real, gap_real = reals[1] + reals[3], reals[1] - reals[3]
    pair_imag, gap_imag = imags[1] + imags[3], imags[1] - imags[3]
    return (
        [even_real + pair_real, odd_real + gap_imag, even_real - pair_real, odd_real - gap_imag],
        [even_imag + pair_imag, odd_imag - gap_real, even_imag - pair_imag, odd_imag + gap_real],
    )


def reduce_rows(blocks, rows, terms, fetch, factors_at, starts, span, partial):
    inner = blocks * LANES
    outer = span // inner
    unroll = math.gcd(16, outer)

    def reduce_block(block, carry):
        for first in range(0, rows, 8):
            sums = (jnp.zeros((terms, LANES), jnp.float32),) * 32
            for part, start in enumerate(starts):

                def step(at, sums, first=first, part=part, start=start):
                    sums = list(sums)
                    for extra in range(unroll):
                        lane = (at * unroll + extra) * inner + block * LANES
                        factors = factors_at(start + lane, first == 0)
                        for row in range(8):
                            value = fetch(part, first + row, lane)
                            value = jnp.broadcast_to(value, (terms, LANES))
                            for k in range(4):
                                sums[row * 4 + k] += value * factors[k]
                    return tuple(sums)

                sums = lax.fori_loop(0, outer // unroll, step, sums)
            for row in range(8):
                for k in range(4):
                    partial[k, block, first + row] = sums[row * 4 + k]
        return carry

    lax.fori_loop(0, blocks, reduce_block, 0)


def transform_rows(blocks, rows, row_at, row_factors, twiddle, table, out, partial, joined):
    terms, total_rows = row_factors[0].shape
    lanes = lax.broadcasted_iota(jnp.int32, (terms, total_rows), 1)

    def butterfly(row, side):
        picked = jnp.where(lanes == row_at(row), row_factors[side][...], 0.0)
        factor = jnp.sum(picked, axis=1, keepdims=True)
        factor = jnp.broadcast_to(factor, (terms, LANES))
        reals = [partial[2 * side, block, row] * factor for block in range(blocks)]
        imags = [partial[2 * side + 1, block, row] * factor for block in range(blocks)]
        reals, imags = block_fourier(reals, imags)
        for block in range(1, blocks):
            real, imag = reals[block], imags[block]
            cosine, sine = twiddle[block, 0], twiddle[block, 1]
            reals[block] = real * cosine - imag * sine
            imags[block] = real * sine + imag * cosine
        return reals, imags

    def butterfly_pair(pair):
        for side in range(2):
            both = [butterfly(pair * 2 + extra, side) for extra in range(2)]
            for block in range(blocks):
                base = ((block * 2 + side) * rows + pair * 2) * terms
                place = pl.ds(base, 2 * terms)
                for part in range(2):
                    values = jnp.concatenate([both[0][part][block], both[1][part][block]], axis=0)
                    high, low = split_parts(values)
                    for third, piece in enumerate((high, low, high)):
                        joined[place, pl.ds((third * 2 + part) * LANES, LANES)] = piece

    for pair in range(rows // 2):
        butterfly_pair(pair)
    planes = 2 * blocks
    step = planes * rows * terms
    while step > 512:
        step //= 2
    plane_step = step // (rows * terms)

    def transform(at, carry):
        place = pl.ds(pl.multiple_of(at * step, 16), step)
        total = jnp.dot(joined[place, :], table[...], preferred_element_type=jnp.float32)
        total = total.reshape(plane_step, rows, terms, 2 * LANES)
        place = pl.ds(at * plane_step, plane_step)
        out[place, 0] = total[..., :LANES]
        out[place, 1] = total[..., LANES:]
        return carry

    lax.fori_loop(0, planes // plane_step, transform, 0)


def comp_of(step, flipped):
    lines = lax.axis_size("comp") // 2
    comp_at = lax.axis_index("comp")
    line = lax.rem(lax.div(comp_at, 2) + lines - step, lines)
    side = lax.rem(comp_at, 2)
    return line * 2 + (1 - side if flipped else side)


def make_phases(groups, phases):
    width = phases.shape[1] * LANES
    device_at = lax.axis_index("comp") * lax.axis_size("rank") + lax.axis_index("rank")
    odd = 4 * lax.rem(device_at, groups) + 1
    shape = phases.shape[1:]
    cells = lax.broadcasted_iota(jnp.int32, shape, 0) * LANES
    cells = cells + lax.broadcasted_iota(jnp.int32, shape, 1)
    turns = (cells * odd) & (4 * width - 1)
    turns = jnp.where(turns >= 2 * width, turns - 4 * width, turns)
    angles = turns.astype(jnp.float32) * (2.0 * math.pi / (4 * width))
    phases[0] = jnp.cos(angles)
    phases[1] = -jnp.sin(angles)


def made_factors(columns, phases, kept):
    terms = columns[0].shape[0]

    def factors_at(lane, first):
        place = pl.ds(pl.multiple_of(lane, LANES), LANES)
        if not first:
            return [kept[k, :, place] for k in range(4)]
        turn = pl.ds(lax.div(lane, LANES), 1)
        factors = [
            column[:, place] * jnp.broadcast_to(phases[part, turn, :], (terms, LANES))
            for column in columns
            for part in range(2)
        ]
        for k in range(4):
            kept[k, :, place] = factors[k]
        return factors

    return factors_at


def start_tables(tables, held, arrivals):
    copies = [
        pltpu.make_async_copy(table, place, arrivals.at[k])
        for k, (table, place) in enumerate(zip(tables, held))
    ]
    for copy in copies:
        copy.start()
    return copies


def pieces_kernel(blocks, groups, sources, count, *refs):
    pieces, refs = refs[:count], refs[count:]
    columns, row_factors, tables, refs = refs[0:2], refs[2:4], refs[4:6], refs[6:]
    out, partial, joined, phases, weights, twiddle, table, arrivals = refs
    copies = start_tables(tables, (twiddle, table), arrivals)
    make_phases(groups, phases)
    rows_here = pieces[0].shape[-2]
    terms, width = columns[0].shape
    ranks = lax.axis_size("rank")
    span = width // ranks
    rank_at = lax.axis_index("rank")
    starts = [(rank_at ^ other) * span for other in HELD_PARTS]
    rows = len(sources) * rows_here

    def fetch(part, row, lane):
        quarters, index, _, _ = sources[row // rows_here]
        row = pl.ds(row % rows_here, 1)
        ref = pieces[quarters[part]]
        if index is None:
            return ref[row, pl.ds(pl.multiple_of(starts[part] + lane, LANES), LANES)]
        return ref[index, row, pl.ds(pl.multiple_of(lane, LANES), LANES)]

    bases = [comp_of(step, flipped) * rows_here for _, _, step, flipped in sources]

    def row_at(row):
        return bases[row // rows_here] + row % rows_here

    factors_at = made_factors(columns, phases, weights)
    reduce_rows(blocks, rows, terms, fetch, factors_at, starts, span, partial)
    for copy in copies:
        copy.wait()
    transform_rows(blocks, rows, row_at, row_factors, twiddle, table, out, partial, joined)


def gathered_kernel(blocks, groups, pieces, *refs):
    columns, row_factors, tables, refs = refs[0:2], refs[2:4], refs[4:6], refs[6:]
    out, partial, joined, phases, weights, twiddle, table, arrivals = refs
    copies = start_tables(tables, (twiddle, table), arrivals)
    make_phases(groups, phases)
    parts, rows_here, span = pieces.shape[1:]

    def fetch(part, row, lane):
        place = pl.ds(pl.multiple_of(lane, LANES), LANES)
        return pieces[row // rows_here, part, pl.ds(row % rows_here, 1), place]

    base = pl.program_id(0) * 8
    starts = [part * span for part in range(parts)]
    terms = columns[0].shape[0]
    factors_at = made_factors(columns, phases, weights)
    reduce_rows(blocks, 8, terms, fetch, factors_at, starts, span, partial)
    for copy in copies:
        copy.wait()
    transform_rows(
        blocks,
        8,
        lambda row: base + row,
        row_factors,
        twiddle,
        table,
        out.at[0],
        partial,
        joined,
    )


def pass_kernel(value, earlier, out):
    del value, earlier, out


def after(value, earlier):
    anywhere = pl.BlockSpec(memory_space=pl.ANY)
    return pl.pallas_call(
        pass_kernel,
        out_shape=jax.ShapeDtypeStruct(value.shape, value.dtype),
        in_specs=[anywhere, anywhere],
        out_specs=anywhere,
        input_output_aliases={0: 0},
    )(*[pltpu.with_memory_space_constraint(array, pltpu.VMEM) for array in (value, earlier)])


def convolve_kernel(blocks, rows_here, layout, tile_count, *refs):
    tiles = refs[:tile_count]
    back, out, spectrum, product, mixed = refs[tile_count:]
    total_rows = spectrum.shape[2] - PAD
    terms = spectrum.shape[3]
    spectrum[:, :, pl.ds(0, PAD)] = jnp.zeros((2 * blocks, 3, PAD, terms, LANES), jnp.float32)
    moves = []
    for number, tile in enumerate(tiles):
        for at in range(tile.shape[0]):
            for first in range(0, tile.shape[3], rows_here):
                moves.append((tile, at, first))
    comps = [comp_of(*layout[k]) if layout else k for k in range(len(moves))]

    def collect(plane, carry):
        for (tile, at, first), comp in zip(moves, comps):
            real = tile[at, plane, 0, pl.ds(first, rows_here)]
            imag = tile[at, plane, 1, pl.ds(first, rows_here)]
            place = pl.ds(PAD + comp * rows_here, rows_here)
            spectrum[plane, 0, place] = real
            spectrum[plane, 1, place] = imag
            spectrum[plane, 2, place] = real + imag
        return carry

    lax.fori_loop(0, 2 * blocks, collect, 0)

    def step(at, sums, block, out_tile, whole):
        sums = list(sums)
        left_base = PAD + 4 * at
        right_base = PAD + 4 * (out_tile - at)
        for part in range(3):
            left = [spectrum[2 * block, part, left_base + k] for k in range(4)]
            right = {
                k: spectrum[2 * block + 1, part, right_base + k]
                for k in range(-3 if whole else 0, 4)
            }
            for row in range(4):
                for k in range(4 if whole else row + 1):
                    sums[row * 3 + part] += left[k] * right[row - k]
        return tuple(sums)

    def finish(sums, block, out_tile):
        for row in range(4):
            both_real, both_imag, crossed = sums[row * 3 : row * 3 + 3]
            base = (out_tile * 4 + row) * 2 * blocks + block
            product[base] = both_real - both_imag
            product[base + blocks] = crossed - both_real - both_imag

    zeros = (jnp.zeros((terms, LANES), jnp.float32),) * 12
    out_tiles = total_rows // 4

    def convolve_block(block, carry):
        for out_tile in range(out_tiles):
            sums = zeros
            for at in range(out_tile + 1):
                sums = step(at, sums, block, out_tile, at < out_tile)
            finish(sums, block, out_tile)
        return carry

    def convolve_tile(index, carry):
        block = lax.rem(index, blocks)
        out_tile = lax.div(index, blocks)
        sums = lax.fori_loop(
            0, out_tile + 1, lambda at, sums: step(at, sums, block, out_tile, True), zeros
        )
        finish(sums, block, out_tile)
        return carry

    if total_rows <= 32:
        lax.fori_loop(0, blocks, convolve_block, 0)
    else:
        lax.fori_loop(0, out_tiles * blocks, convolve_tile, 0)

    def gather_terms(at, carry):
        tiles = [product[at * 8 + k] for k in range(8)]
        summed = jnp.sum(jnp.stack(tiles), axis=1)
        if blocks == 4:
            turned = jnp.concatenate([summed[blocks:], -summed[:blocks]], axis=0)
        else:
            swapped = [
                tiles[k + blocks] if (k // blocks) % 2 == 0 else -tiles[k - blocks]
                for k in range(8)
            ]
            turned = jnp.sum(jnp.stack(swapped), axis=1)
        place = pl.ds(pl.multiple_of(at * 8, 8), 8)
        mixed[place, pl.ds(0, LANES)] = summed
        mixed[place, pl.ds(LANES, LANES)] = turned
        return carry

    lax.fori_loop(0, total_rows * 2 * blocks // 8, gather_terms, 0, unroll=4)
    out[...] = dot_split(mixed[...], back[...])


def final_kernel(scaling, spread, inner_cos, inner_sin, outer, out):
    values = spread[...]
    stacked = jnp.concatenate([values * inner_cos[...], values * inner_sin[...]], axis=0)
    high, low = split_parts(stacked)
    joined = jnp.concatenate([high, low, high], axis=0)
    total = jnp.dot(outer[...], joined, preferred_element_type=jnp.float32)
    out[...] = total * scaling


def whole_call(kernel, out_shapes, scratch, operands, tables=(), kept=True):
    out_type = pltpu.VMEM if kept else jax.ShapeDtypeStruct
    operands = [pltpu.with_memory_space_constraint(operand, pltpu.VMEM) for operand in operands]
    return pl.pallas_call(
        kernel,
        out_shape=[out_type(shape, jnp.float32) for shape in out_shapes],
        in_specs=[pl.BlockSpec(memory_space=pltpu.VMEM)] * len(operands)
        + [pl.BlockSpec(memory_space=pl.ANY)] * len(tables),
        out_specs=[pl.BlockSpec(memory_space=pltpu.VMEM)] * len(out_shapes),
        scratch_shapes=scratch,
        compiler_params=pltpu.CompilerParams(vmem_limit_bytes=VMEM_BYTES),
    )(*operands, *tables)


def row_scratch(blocks, rows, terms, width, tables):
    return [
        pltpu.VMEM((4, blocks, rows, terms, LANES), jnp.float32),
        pltpu.VMEM((2 * blocks * rows * terms, 6 * LANES), jnp.bfloat16),
        pltpu.VMEM((2, width // LANES, LANES), jnp.float32),
        pltpu.VMEM((4, terms, width), jnp.float32),
        *[pltpu.VMEM(table.shape, table.dtype) for table in tables],
        pltpu.SemaphoreType.DMA((len(tables),)),
    ]


def spectra_by_exchange(density, blocks, groups, columns, row_factors, tables):
    rows_here, width = density.shape
    comps, ranks = lax.axis_size("comp"), lax.axis_size("rank")
    part = width // ranks
    lines = comps // 2
    terms = row_factors[0].shape[0]
    mine = lax.dynamic_slice_in_dim(density, lax.axis_index("rank") * part, part, 1)

    def along(block, step):
        pairs = [(c, ((c // 2 + step) % lines) * 2 + c % 2) for c in range(comps)]
        return lax.ppermute(block, "comp", pairs)

    def across(block):
        return lax.ppermute(block, "comp", [(c, c ^ 1) for c in range(comps)])

    def swapped(block, other):
        return lax.ppermute(block, "rank", [(r, r ^ other) for r in range(ranks)])

    def spectra(pieces, sources):
        rows = rows_here * len(sources)
        (tile,) = whole_call(
            lambda *refs: pieces_kernel(blocks, groups, sources, len(pieces), *refs),
            [(2 * blocks, 2, rows, terms, LANES)],
            row_scratch(blocks, rows, terms, width, tables),
            (*pieces, *columns, *row_factors),
            tables,
        )
        return tile

    lined = [along(mine, step) for step in range(1, lines)]
    flipped_own = across(mine)
    line_near = jnp.stack(lined)
    near = jnp.concatenate([flipped_own[None], line_near])
    flipped_near = across(line_near)
    near_beyond = swapped(near, 2)
    ready = [near, near_beyond, swapped(near, 1), swapped(near_beyond, 1)]
    flipped_beyond = swapped(flipped_near, 2)
    flipped_beside = swapped(flipped_near, 1)

    quarters = (1, 2, 3, 4)
    early = [((0, 0, 0, 0), None, 0, False), (quarters, 0, 0, True)]
    early += [(quarters, step, step, False) for step in range(1, lines)]
    late = early[comps // 2 :]
    early = early[: comps // 2]
    first = spectra([density, *ready], early)
    flipped_beyond = after(flipped_beyond, first)
    flipped = [flipped_near, flipped_beyond, flipped_beside, swapped(flipped_beyond, 1)]
    late = [((0, 1, 2, 3), *rest) for _, *rest in late]
    late += [((4, 5, 6, 7), step - 1, step, True) for step in range(1, lines)]
    second = spectra([*ready, *flipped], late)
    layout = [source[2:] for source in early + late]
    return [first[None], second[None]], layout


def spectra_by_gather(density, blocks, groups, columns, row_factors, tables):
    rows_here, width = density.shape
    comps, ranks = lax.axis_size("comp"), lax.axis_size("rank")
    terms = row_factors[0].shape[0]
    total_rows = rows_here * comps
    part = width // ranks
    mine = lax.dynamic_slice_in_dim(density, lax.axis_index("rank") * part, part, 1)
    gathered = lax.all_gather(mine, AXES, axis=0).reshape(comps, ranks, rows_here, part)
    tile_shape = (2 * blocks, 2, 8, terms, LANES)
    spectra = pl.pallas_call(
        lambda *refs: gathered_kernel(blocks, groups, *refs),
        grid=(total_rows // 8,),
        out_shape=jax.ShapeDtypeStruct((total_rows // 8, *tile_shape), jnp.float32),
        in_specs=[pl.BlockSpec((8 // rows_here, ranks, rows_here, part), lambda t: (t, 0, 0, 0))]
        + [pl.BlockSpec(memory_space=pltpu.VMEM)] * 4
        + [pl.BlockSpec(memory_space=pl.ANY)] * len(tables),
        out_specs=pl.BlockSpec((1, *tile_shape), lambda t: (t, 0, 0, 0, 0, 0)),
        scratch_shapes=row_scratch(blocks, 8, terms, width, tables),
        compiler_params=pltpu.CompilerParams(vmem_limit_bytes=VMEM_BYTES),
    )(gathered, *columns, *row_factors, *tables)
    return [spectra], None


def body(density, row_left, col_left, row_right, col_right):
    rows_here, width = density.shape
    comps = lax.axis_size("comp")
    devices = comps * lax.axis_size("rank")
    total_rows = rows_here * comps
    terms = row_left.shape[0]
    groups = min(devices, width // LANES)
    term_groups = devices // groups
    blocks = width // (groups * LANES)
    device_at = lax.axis_index(AXES)
    if term_groups > 1:
        term_at = lax.broadcasted_iota(jnp.int32, (terms, 1), 0)
        chosen = lax.div(term_at, terms // term_groups) == lax.div(device_at, groups)
        col_left = jnp.where(chosen, col_left, 0.0)
        col_right = jnp.where(chosen, col_right, 0.0)
    columns = (col_left, col_right)
    row_factors = (row_left, row_right)
    tables = (block_twiddles(blocks), split_rows(forward_table()))
    spectra = spectra_by_exchange if comps <= 8 else spectra_by_gather
    tiles, layout = spectra(density, blocks, groups, columns, row_factors, tables)

    out_rows = total_rows * 2 * blocks
    (sent,) = whole_call(
        lambda *refs: convolve_kernel(blocks, rows_here, layout, len(tiles), *refs),
        [(out_rows, LANES)],
        [
            pltpu.VMEM((2 * blocks, 3, PAD + total_rows, terms, LANES), jnp.float32),
            pltpu.VMEM((out_rows, terms, LANES), jnp.float32),
            pltpu.VMEM((out_rows, 2 * LANES), jnp.float32),
        ],
        (*tiles, split_rows(inverse_table())),
    )
    spread = lax.all_to_all(sent, AXES, split_axis=0, concat_axis=0, tiled=True)
    inner_cos, inner_sin, outer_table = final_tables(devices, groups, blocks, width)
    scaling = 0.5 / (math.sqrt(total_rows * width) * width)
    (result,) = whole_call(
        lambda *refs: final_kernel(scaling, *refs),
        [(width // LANES, LANES)],
        [],
        (
            spread,
            jnp.asarray(inner_cos, jnp.float32),
            jnp.asarray(inner_sin, jnp.float32),
            split_columns(outer_table),
        ),
        kept=False,
    )
    return result.reshape(1, width)


def solution(mesh):
    return jax.shard_map(
        body,
        mesh=mesh,
        in_specs=(P("comp", None), P(), P(), P(), P()),
        out_specs=P(AXES, None),
        check_vma=False,
    )
```

profile of v0, /device:TPU:0, one launch (start us, length us, event | category | flops | bytes accessed | tf_op | source)
XLA Modules:
  0.0 52.6 jit_solution(6275445149390743602)
XLA Ops:
  0.0 0.9 %constant_dynamic-slice_fusion = f32[4,4096]{1,0:T(4,128)S(1)} fusion(f32[4,16384]{1,0:T(4,128)} %refs_0_.1, s32[]{:T(128)S(6)} %select_n.3), kind=kLoop, calls=%fused_computation.2 | loop fusion | bytes 131076 | tf_op jit(solution)/shard_map/dynamic_slice | solution.py:441
  0.9 5.0 %collective-permute-start.3 = (f32[4,4096]{1,0:T(4,128)S(1)}, f32[4,4096]{1,0:T(4,128)S(1)}, u32[]{:S(2)}, u32[]{:S(2)}) collective-permute-start(f32[4,4096]{1,0:T(4,128)S(1)} %constant_dynamic-slice_fusion), channel_id=1, source_target_pairs={{0,24},{4,28},{8,0},{12,4},{16,8},{20,12},{24,16},{28,20},{1,25},{... | collective-permute-start | bytes 196616 | tf_op jit(solution)/shard_map/ppermute | solution.py:445
  6.0 0.0 collective-permute-start.2
  6.0 1.0 %collective-permute-start.1 = (f32[4,4096]{1,0:T(4,128)S(1)}, f32[4,4096]{1,0:T(4,128)S(1)}, u32[]{:S(2)}, u32[]{:S(2)}) collective-permute-start(f32[4,4096]{1,0:T(4,128)S(1)} %constant_dynamic-slice_fusion), channel_id=1, source_target_pairs={{0,8},{4,12},{8,16},{12,20},{16,24},{20,28},{24,0},{28,4},{1,9},{5... | collective-permute-start | bytes 196616 | tf_op jit(solution)/shard_map/ppermute | solution.py:445
  7.0 1.5 %collective-permute-start = (f32[4,4096]{1,0:T(4,128)S(1)}, f32[4,4096]{1,0:T(4,128)S(1)}, u32[]{:S(2)}, u32[]{:S(2)}) collective-permute-start(f32[4,4096]{1,0:T(4,128)S(1)} %constant_dynamic-slice_fusion), channel_id=1, source_target_pairs={{0,4},{4,0},{8,12},{12,8},{16,20},{20,16},{24,28},{28,24},{1,5},{5... | collective-permute-start | bytes 196616 | tf_op jit(solution)/shard_map/ppermute | solution.py:448
  8.5 0.0 collective-permute-done.3
  8.5 3.9 %collective-permute-done.2 = f32[4,4096]{1,0:T(4,128)S(1)} collective-permute-done((f32[4,4096]{1,0:T(4,128)S(1)}, f32[4,4096]{1,0:T(4,128)S(1)}, u32[]{:S(2)}, u32[]{:S(2)}) %collective-permute-start.2) | collective-permute-done | bytes 65568 | tf_op jit(solution)/shard_map/ppermute | solution.py:445
  12.5 0.0 collective-permute-done.1
  12.5 0.0 collective-permute-done
  12.5 0.1 pad_maximum_fusion.refs_1_.refs_0_
  12.5 0.0 copy-start.13
  12.5 0.0 copy-start.14
  12.6 1.6 %collective-permute-start.4 = (f32[4,4,4096]{2,1,0:T(4,128)S(1)}, f32[4,4,4096]{2,1,0:T(4,128)S(1)}, u32[]{:S(2)}, u32[]{:S(2)}) collective-permute-start(f32[4,4,4096]{2,1,0:T(4,128)S(1)} %pad_maximum_fusion.refs_1_.refs_0_), channel_id=1, source_target_pairs={{0,2},{1,3},{2,0},{3,1},{4,6},{5,7},{6,4},{7,5},{8,10},{9,11},{10,... | collective-permute-start | bytes 786440 | tf_op jit(solution)/shard_map/ppermute | solution.py:451
  14.2 1.6 %collective-permute-start.7 = (f32[3,4,4096]{2,1,0:T(4,128)S(1)}, f32[3,4,4096]{2,1,0:T(4,128)}, u32[]{:S(2)}, u32[]{:S(2)}) collective-permute-start(f32[3,4,4096]{2,1,0:T(4,128)S(1)} %pad_maximum_fusion.1), channel_id=1, source_target_pairs={{0,4},{4,0},{8,12},{12,8},{16,20},{20,16},{24,28},{28,24},{1,5},{5... | collective-permute-start | bytes 589832 | tf_op jit(solution)/shard_map/ppermute | solution.py:448
  15.7 0.0 collective-permute-start.5
  15.7 4.9 %collective-permute-done.4.refs_2_.refs_1_ = f32[4,4,4096]{2,1,0:T(4,128)S(1)} collective-permute-done((f32[4,4,4096]{2,1,0:T(4,128)S(1)}, f32[4,4,4096]{2,1,0:T(4,128)S(1)}, u32[]{:S(2)}, u32[]{:S(2)}) %collective-permute-start.4) | collective-permute-done | bytes 262176 | tf_op jit(solution)/shard_map/ppermute | solution.py:451
  20.7 0.0 collective-permute-start.6
  20.7 0.0 collective-permute-done.7.refs_4_
  20.7 1.5 %collective-permute-start.8 = (f32[3,4,4096]{2,1,0:T(4,128)}, f32[3,4,4096]{2,1,0:T(4,128)S(1)}, u32[]{:S(2)}, u32[]{:S(2)}) collective-permute-start(f32[3,4,4096]{2,1,0:T(4,128)} %collective-permute-done.7.refs_4_), channel_id=1, source_target_pairs={{0,2},{1,3},{2,0},{3,1},{4,6},{5,7},{6,4},{7,5},{8,10},{9,11},{10,... | collective-permute-start | bytes 589832 | tf_op jit(solution)/shard_map/ppermute | solution.py:451
  22.2 0.2 collective-permute-start.9
  22.4 0.0 collective-permute-done.5.refs_3_.refs_2_
  22.4 0.0 collective-permute-done.6.refs_4_.refs_3_
  22.4 0.0 copy-done
  22.4 0.0 copy-done.1
  22.4 0.0 copy-done.13
  22.4 0.0 copy-done.14
  22.4 0.0 copy-start.2
  22.4 1.0 %copy-done.2 = bf16[768,256]{1,0:T(8,128)(2,1)S(1)} copy-done((bf16[768,256]{1,0:T(8,128)(2,1)S(1)}, bf16[768,256]{1,0:T(8,128)(2,1)}, u32[]{:S(2)}) %copy-start.2) | copy-done | bytes 393240
  23.4 0.9 %copy-done.6 = f32[4,16384]{1,0:T(4,128)S(1)} copy-done((f32[4,16384]{1,0:T(4,128)S(1)}, f32[4,16384]{1,0:T(4,128)}, u32[]{:S(2)}) %copy-start.6) | copy-done | bytes 262168
  24.4 0.8 %copy-done.9 = f32[4,2,8,128]{3,2,1,0:T(8,128)S(1)} copy-done((f32[4,2,8,128]{3,2,1,0:T(8,128)S(1)}, f32[4,2,8,128]{3,2,1,0:T(8,128)}, u32[]{:S(2)}) %copy-start.9) | copy-done | bytes 32792
  25.1 4.0 %shard_map.109.earlier = f32[8,2,16,8,128]{4,3,2,1,0:T(8,128)S(1)} custom-call(f32[4,16384]{1,0:T(4,128)S(1)} %copy-done.6, f32[4,4,4096]{2,1,0:T(4,128)S(1)} %pad_maximum_fusion.refs_1_.refs_0_, f32[4,4,4096]{2,1,0:T(4,128)S(1)} %collective-permute-done.4.refs_2_.refs_1_, f32[4,4,4096]{2,1,0:T(4,128)S(1)} %collective-permute-done.5.refs_3_.refs_2_, ...), custom_call_target="tpu_custom_call" | custom-call | tf_op jit(solution)/shard_map/pallas_call | solution.py:413
  29.1 0.0 copy-start.4
  29.1 0.7 %copy-done.4 = f32[4,4,4096]{2,1,0:T(4,128)} copy-done((f32[4,4,4096]{2,1,0:T(4,128)}, f32[4,4,4096]{2,1,0:T(4,128)S(1)}, u32[]{:S(2)}) %copy-start.4) | copy-done | bytes 262168
  29.8 0.0 collective-permute-done.8.value
  29.8 0.3 collective-permute-start.10
  30.2 0.0 collective-permute-done.9.refs_6_
  30.2 1.2 %collective-permute-done.10.refs_7_ = f32[3,4,4096]{2,1,0:T(4,128)S(1)} collective-permute-done((f32[3,4,4096]{2,1,0:T(4,128)S(1)}, f32[3,4,4096]{2,1,0:T(4,128)S(1)}, u32[]{:S(2)}, u32[]{:S(2)}) %collective-permute-start.10) | collective-permute-done | bytes 196640 | tf_op jit(solution)/shard_map/ppermute | solution.py:451
  31.3 0.0 copy-done.3
  31.3 0.0 copy-done.10
  31.3 0.9 %copy-done.5 = f32[4,4,4096]{2,1,0:T(4,128)S(1)} copy-done((f32[4,4,4096]{2,1,0:T(4,128)S(1)}, f32[4,4,4096]{2,1,0:T(4,128)}, u32[]{:S(2)}) %copy-start.5) | copy-done | bytes 262168
  32.3 5.0 %shard_map.111 = f32[8,2,16,8,128]{4,3,2,1,0:T(8,128)S(1)} custom-call(f32[4,4,4096]{2,1,0:T(4,128)S(1)} %pad_maximum_fusion.refs_1_.refs_0_, f32[4,4,4096]{2,1,0:T(4,128)S(1)} %collective-permute-done.4.refs_2_.refs_1_, f32[4,4,4096]{2,1,0:T(4,128)S(1)} %collective-permute-done.5.refs_3_.refs_2_, f32[4,4,4096]{2,1,0:T(4,128)S(1)} %copy-done.5, ...), custom_call_target="tpu_custom_call" | custom-call | tf_op jit(solution)/shard_map/pallas_call | solution.py:413
  37.3 0.0 copy-start.7
  37.3 2.9 %shard_map.112 = f32[256,128]{1,0:T(8,128)S(1)} custom-call(f32[1,8,2,16,8,128]{5,4,3,2,1,0:T(8,128)S(1)} %bitcast.9, f32[1,8,2,16,8,128]{5,4,3,2,1,0:T(8,128)S(1)} %bitcast.10, bf16[768,128]{1,0:T(8,128)(2,1)S(1)} %copy-done.8), custom_call_target="tpu_custom_call" | custom-call | tf_op jit(solution)/shard_map/pallas_call | solution.py:413
  40.2 0.0 copy-start.11
  40.2 0.0 copy-start.12
  40.2 11.5 %all_to_all.11 = f32[32,8,128]{2,1,0:T(8,128)S(1)} all-to-all(f32[32,8,128]{2,1,0:T(8,128)S(1)} %bitcast.11), channel_id=1, replica_groups=mesh['comp'=8,'rank'=4] {'comp','rank'}, dimensions={0} | all-to-all | bytes 262144 | tf_op jit(solution)/shard_map/all_to_all | solution.py:544
  51.7 0.0 copy-done.11
  51.7 0.9 %shard_map.113 = f32[128,128]{1,0:T(8,128)} custom-call(f32[256,128]{1,0:T(8,128)S(1)} %bitcast.12, f32[256,128]{1,0:T(8,128)S(1)} %copy-done.12, f32[256,128]{1,0:T(8,128)S(1)} %copy-done.11, bf16[128,1536]{1,0:T(8,128)(2,1)S(1)} %copy-done.7), custom_call_target="tpu_custom_call" | custom-call | tf_op jit(solution)/shard_map/pallas_call | solution.py:413
  (13 shorter events, 0.1 us)
Async XLA Ops:
  0.0 22.4 %copy-start = (f32[8,16384]{1,0:T(8,128)S(1)}, f32[8,16384]{1,0:T(8,128)}, u32[]{:S(2)}) copy-start(f32[8,16384]{1,0:T(8,128)} %refs_8_.3) | copy-start | bytes 1572868
  0.0 22.4 %copy-start.1 = (f32[8,16384]{1,0:T(8,128)S(1)}, f32[8,16384]{1,0:T(8,128)}, u32[]{:S(2)}) copy-start(f32[8,16384]{1,0:T(8,128)} %refs_9_.2) | copy-start | bytes 1572868
  0.9 7.6 %collective-permute-start.3 = (f32[4,4096]{1,0:T(4,128)S(1)}, f32[4,4096]{1,0:T(4,128)S(1)}, u32[]{:S(2)}, u32[]{:S(2)}) collective-permute-start(f32[4,4096]{1,0:T(4,128)S(1)} %constant_dynamic-slice_fusion), channel_id=1, source_target_pairs={{0,24},{4,28},{8,0},{12,4},{16,8},{20,12},{24,16},{28,20},{1,25},{... | collective-permute-start | bytes 196616 | tf_op jit(solution)/shard_map/ppermute | solution.py:445
  6.0 6.5 %collective-permute-start.2 = (f32[4,4096]{1,0:T(4,128)S(1)}, f32[4,4096]{1,0:T(4,128)S(1)}, u32[]{:S(2)}, u32[]{:S(2)}) collective-permute-start(f32[4,4096]{1,0:T(4,128)S(1)} %constant_dynamic-slice_fusion), channel_id=1, source_target_pairs={{0,16},{4,20},{8,24},{12,28},{16,0},{20,4},{24,8},{28,12},{1,17},{... | collective-permute-start | bytes 196616 | tf_op jit(solution)/shard_map/ppermute | solution.py:445
  6.0 6.5 %collective-permute-start.1 = (f32[4,4096]{1,0:T(4,128)S(1)}, f32[4,4096]{1,0:T(4,128)S(1)}, u32[]{:S(2)}, u32[]{:S(2)}) collective-permute-start(f32[4,4096]{1,0:T(4,128)S(1)} %constant_dynamic-slice_fusion), channel_id=1, source_target_pairs={{0,8},{4,12},{8,16},{12,20},{16,24},{20,28},{24,0},{28,4},{1,9},{5... | collective-permute-start | bytes 196616 | tf_op jit(solution)/shard_map/ppermute | solution.py:445
  7.0 5.5 %collective-permute-start = (f32[4,4096]{1,0:T(4,128)S(1)}, f32[4,4096]{1,0:T(4,128)S(1)}, u32[]{:S(2)}, u32[]{:S(2)}) collective-permute-start(f32[4,4096]{1,0:T(4,128)S(1)} %constant_dynamic-slice_fusion), channel_id=1, source_target_pairs={{0,4},{4,0},{8,12},{12,8},{16,20},{20,16},{24,28},{28,24},{1,5},{5... | collective-permute-start | bytes 196616 | tf_op jit(solution)/shard_map/ppermute | solution.py:448
  12.5 9.9 %copy-start.13 = (f32[8,32]{1,0:T(8,128)S(1)}, f32[8,32]{1,0:T(8,128)}, u32[]{:S(2)}) copy-start(f32[8,32]{1,0:T(8,128)} %refs_10_.1) | copy-start | bytes 3076
  12.5 9.9 %copy-start.14 = (f32[8,32]{1,0:T(8,128)S(1)}, f32[8,32]{1,0:T(8,128)}, u32[]{:S(2)}) copy-start(f32[8,32]{1,0:T(8,128)} %refs_11_.1) | copy-start | bytes 3076
  12.6 8.1 %collective-permute-start.4 = (f32[4,4,4096]{2,1,0:T(4,128)S(1)}, f32[4,4,4096]{2,1,0:T(4,128)S(1)}, u32[]{:S(2)}, u32[]{:S(2)}) collective-permute-start(f32[4,4,4096]{2,1,0:T(4,128)S(1)} %pad_maximum_fusion.refs_1_.refs_0_), channel_id=1, source_target_pairs={{0,2},{1,3},{2,0},{3,1},{4,6},{5,7},{6,4},{7,5},{8,10},{9,11},{10,... | collective-permute-start | bytes 786440 | tf_op jit(solution)/shard_map/ppermute | solution.py:451
  14.2 6.5 %collective-permute-start.7 = (f32[3,4,4096]{2,1,0:T(4,128)S(1)}, f32[3,4,4096]{2,1,0:T(4,128)}, u32[]{:S(2)}, u32[]{:S(2)}) collective-permute-start(f32[3,4,4096]{2,1,0:T(4,128)S(1)} %pad_maximum_fusion.1), channel_id=1, source_target_pairs={{0,4},{4,0},{8,12},{12,8},{16,20},{20,16},{24,28},{28,24},{1,5},{5... | collective-permute-start | bytes 589832 | tf_op jit(solution)/shard_map/ppermute | solution.py:448
  15.7 6.6 %collective-permute-start.5 = (f32[4,4,4096]{2,1,0:T(4,128)S(1)}, f32[4,4,4096]{2,1,0:T(4,128)S(1)}, u32[]{:S(2)}, u32[]{:S(2)}) collective-permute-start(f32[4,4,4096]{2,1,0:T(4,128)S(1)} %pad_maximum_fusion.refs_1_.refs_0_), channel_id=1, source_target_pairs={{0,1},{1,0},{2,3},{3,2},{4,5},{5,4},{6,7},{7,6},{8,9},{9,8},{10,11... | collective-permute-start | bytes 786440 | tf_op jit(solution)/shard_map/ppermute | solution.py:451
  20.7 1.7 %collective-permute-start.6 = (f32[4,4,4096]{2,1,0:T(4,128)S(1)}, f32[4,4,4096]{2,1,0:T(4,128)S(1)}, u32[]{:S(2)}, u32[]{:S(2)}) collective-permute-start(f32[4,4,4096]{2,1,0:T(4,128)S(1)} %collective-permute-done.4.refs_2_.refs_1_), channel_id=1, source_target_pairs={{0,1},{1,0},{2,3},{3,2},{4,5},{5,4},{6,7},{7,6},{8,9},{9,8},{10,11... | collective-permute-start | bytes 786440 | tf_op jit(solution)/shard_map/ppermute | solution.py:451
  20.7 9.1 %collective-permute-start.8 = (f32[3,4,4096]{2,1,0:T(4,128)}, f32[3,4,4096]{2,1,0:T(4,128)S(1)}, u32[]{:S(2)}, u32[]{:S(2)}) collective-permute-start(f32[3,4,4096]{2,1,0:T(4,128)} %collective-permute-done.7.refs_4_), channel_id=1, source_target_pairs={{0,2},{1,3},{2,0},{3,1},{4,6},{5,7},{6,4},{7,5},{8,10},{9,11},{10,... | collective-permute-start | bytes 589832 | tf_op jit(solution)/shard_map/ppermute | solution.py:451
  22.2 8.0 %collective-permute-start.9 = (f32[3,4,4096]{2,1,0:T(4,128)}, f32[3,4,4096]{2,1,0:T(4,128)}, u32[]{:S(2)}, u32[]{:S(2)}) collective-permute-start(f32[3,4,4096]{2,1,0:T(4,128)} %collective-permute-done.7.refs_4_), channel_id=1, source_target_pairs={{0,1},{1,0},{2,3},{3,2},{4,5},{5,4},{6,7},{7,6},{8,9},{9,8},{10,11... | collective-permute-start | bytes 589832 | tf_op jit(solution)/shard_map/ppermute | solution.py:451
  22.4 1.0 %copy-start.2 = (bf16[768,256]{1,0:T(8,128)(2,1)S(1)}, bf16[768,256]{1,0:T(8,128)(2,1)}, u32[]{:S(2)}) copy-start(bf16[768,256]{1,0:T(8,128)(2,1)} %constant.33.refs_10_.refs_13_) | copy-start | bytes 1179652
  23.4 0.9 %copy-start.6 = (f32[4,16384]{1,0:T(4,128)S(1)}, f32[4,16384]{1,0:T(4,128)}, u32[]{:S(2)}) copy-start(f32[4,16384]{1,0:T(4,128)} %refs_0_.1) | copy-start | bytes 786436
  24.4 0.8 %copy-start.9 = (f32[4,2,8,128]{3,2,1,0:T(8,128)S(1)}, f32[4,2,8,128]{3,2,1,0:T(8,128)}, u32[]{:S(2)}) copy-start(f32[4,2,8,128]{3,2,1,0:T(8,128)} %constant.22.clone.refs_9_.refs_12_) | copy-start | bytes 98308
  29.1 0.7 %copy-start.4 = (f32[4,4,4096]{2,1,0:T(4,128)}, f32[4,4,4096]{2,1,0:T(4,128)S(1)}, u32[]{:S(2)}) copy-start(f32[4,4,4096]{2,1,0:T(4,128)S(1)} %collective-permute-done.6.refs_4_.refs_3_) | copy-start | bytes 786436
  29.8 1.5 %copy-start.3 = (bf16[768,256]{1,0:T(8,128)(2,1)S(1)}, bf16[768,256]{1,0:T(8,128)(2,1)}, u32[]{:S(2)}) copy-start(bf16[768,256]{1,0:T(8,128)(2,1)} %constant.33.refs_10_.refs_13_) | copy-start | bytes 1179652
  29.8 1.5 %copy-start.10 = (f32[4,2,8,128]{3,2,1,0:T(8,128)S(1)}, f32[4,2,8,128]{3,2,1,0:T(8,128)}, u32[]{:S(2)}) copy-start(f32[4,2,8,128]{3,2,1,0:T(8,128)} %constant.22.clone.refs_9_.refs_12_) | copy-start | bytes 98308
  29.8 1.5 %collective-permute-start.10 = (f32[3,4,4096]{2,1,0:T(4,128)S(1)}, f32[3,4,4096]{2,1,0:T(4,128)S(1)}, u32[]{:S(2)}, u32[]{:S(2)}) collective-permute-start(f32[3,4,4096]{2,1,0:T(4,128)S(1)} %shard_map.110.refs_5_), channel_id=1, source_target_pairs={{0,1},{1,0},{2,3},{3,2},{4,5},{5,4},{6,7},{7,6},{8,9},{9,8},{10,11... | collective-permute-start | bytes 589832 | tf_op jit(solution)/shard_map/ppermute | solution.py:451
  31.3 1.0 %copy-start.5 = (f32[4,4,4096]{2,1,0:T(4,128)S(1)}, f32[4,4,4096]{2,1,0:T(4,128)}, u32[]{:S(2)}) copy-start(f32[4,4,4096]{2,1,0:T(4,128)} %copy-done.4) | copy-start | bytes 786436
  32.3 5.0 %copy-start.8 = (bf16[768,128]{1,0:T(8,128)(2,1)S(1)}, bf16[768,128]{1,0:T(8,128)(2,1)}, u32[]{:S(2)}) copy-start(bf16[768,128]{1,0:T(8,128)(2,1)} %constant.38.refs_2_) | copy-start | bytes 589828
  37.3 14.4 %copy-start.7 = (bf16[128,1536]{1,0:T(8,128)(2,1)S(1)}, bf16[128,1536]{1,0:T(8,128)(2,1)}, u32[]{:S(2)}) copy-start(bf16[128,1536]{1,0:T(8,128)(2,1)} %constant.43.refs_3_) | copy-start | bytes 1179652
  40.2 11.5 %copy-start.11 = (f32[256,128]{1,0:T(8,128)S(1)}, f32[256,128]{1,0:T(8,128)}, u32[]{:S(2)}) copy-start(f32[256,128]{1,0:T(8,128)} %constant.26.clone.refs_2_) | copy-start | bytes 393220
  40.2 11.5 %copy-start.12 = (f32[256,128]{1,0:T(8,128)S(1)}, f32[256,128]{1,0:T(8,128)}, u32[]{:S(2)}) copy-start(f32[256,128]{1,0:T(8,128)} %constant.25.clone.refs_1_) | copy-start | bytes 393220
where the time goes:
time: 53 us; the launch traced here: 52.6 us
  starting transfers between devices  12.8 us (24%)
  Pallas kernels  12.7 us (24%)
  blocking collectives  11.5 us (22%)
  waiting for transfers between devices  10 us (19%)
  local copies, waits for them, and re-layouts  5.33 us (10%)
    pallas_call x4, Pallas kernels, whole_call(): pl.pallas_call(kernel, out_shape=[out_type(shape, jnp.float32) for shape...  12.7 us
    all_to_all x1, blocking collectives, body(): spread = lax.all_to_all(sent, AXES, split_axis=0, concat_axis=0, tiled=True)  11.5 us
    ppermute x6, waiting for transfers between devices, swapped(): return lax.ppermute(block, 'rank', [(r, r ^ other) for r in range(ranks)])  6.07 us
    ppermute x3, starting transfers between devices, along(): return lax.ppermute(block, 'comp', pairs)  6.06 us
    unnamed x30, local copies, waits for them, and re-layouts  4.4 us
    ppermute x3, waiting for transfers between devices, along(): return lax.ppermute(block, 'comp', pairs)  3.94 us
    ppermute x6, starting transfers between devices, swapped(): return lax.ppermute(block, 'rank', [(r, r ^ other) for r in range(ranks)])  3.61 us
    ppermute x2, starting transfers between devices, across(): return lax.ppermute(block, 'comp', [(c, c ^ 1) for c in range(comps)])  3.1 us
  transfers between devices with their start and end apart: 11, of which 3 were waited for; matrix products, arithmetic and copies ran while one was open for 0% of the time, Pallas kernels for 8%

commit v1 on v0

--- a/solution.py
+++ b/solution.py
@@ -9,7 +9,7 @@
 from jax.sharding import PartitionSpec as P
 
 LANES = 128
-VMEM_BYTES = 28 * 1024 * 1024
+VMEM_BYTES = 16 * 1024 * 1024
 AXES = ("comp", "rank")
 PAD = 4
 HELD_PARTS = (0, 2, 1, 3)
@@ -98,30 +98,34 @@
     outer = span // inner
     unroll = math.gcd(16, outer)
 
-    def reduce_block(block, carry):
-        for first in range(0, rows, 8):
-            sums = (jnp.zeros((terms, LANES), jnp.float32),) * 32
-            for part, start in enumerate(starts):
-
-                def step(at, sums, first=first, part=part, start=start):
-                    sums = list(sums)
-                    for extra in range(unroll):
-                        lane = (at * unroll + extra) * inner + block * LANES
-                        factors = factors_at(start + lane, first == 0)
-                        for row in range(8):
-                            value = fetch(part, first + row, lane)
-                            value = jnp.broadcast_to(value, (terms, LANES))
-                            for k in range(4):
-                                sums[row * 4 + k] += value * factors[k]
-                    return tuple(sums)
-
-                sums = lax.fori_loop(0, outer // unroll, step, sums)
-            for row in range(8):
-                for k in range(4):
-                    partial[k, block, first + row] = sums[row * 4 + k]
-        return carry
-
-    lax.fori_loop(0, blocks, reduce_block, 0)
+    def reduce_block(block, first, count):
+        sums = (jnp.zeros((terms, LANES), jnp.float32),) * (4 * count)
+        for part, start in enumerate(starts):
+
+            def step(at, sums, part=part, start=start):
+                sums = list(sums)
+                for extra in range(unroll):
+                    lane = (at * unroll + extra) * inner + block * LANES
+                    factors = factors_at(start + lane, first == 0)
+                    for row in range(count):
+                        value = fetch(part, first + row, lane)
+                        value = jnp.broadcast_to(value, (terms, LANES))
+                        for k in range(4):
+                            sums[row * 4 + k] += value * factors[k]
+                return tuple(sums)
+
+            sums = lax.fori_loop(0, outer // unroll, step, sums)
+        for row in range(count):
+            for k in range(4):
+                partial[k, block, first + row] = sums[row * 4 + k]
+
+    for first in range(0, rows, 8):
+
+        def reduce_tile(block, carry, first=first):
+            reduce_block(block, first, min(8, rows - first))
+            return carry
+
+        lax.fori_loop(0, blocks, reduce_tile, 0)
 
 
 def transform_rows(blocks, rows, row_at, row_factors, twiddle, table, out, partial, joined):
@@ -306,7 +310,7 @@
     )(*[pltpu.with_memory_space_constraint(array, pltpu.VMEM) for array in (value, earlier)])
 
 
-def convolve_kernel(blocks, rows_here, layout, tile_count, *refs):
+def convolve_kernel(blocks, rows_here, layout, by_rank, tile_count, *refs):
     tiles = refs[:tile_count]
     back, out, spectrum, product, mixed = refs[tile_count:]
     total_rows = spectrum.shape[2] - PAD
@@ -389,6 +393,9 @@
                 for k in range(8)
             ]
             turned = jnp.sum(jnp.stack(swapped), axis=1)
+        if by_rank:
+            ranks = lax.axis_size("rank")
+            at = lax.rem(at, ranks) * (total_rows // ranks) + lax.div(at, ranks)
         place = pl.ds(pl.multiple_of(at * 8, 8), 8)
         mixed[place, pl.ds(0, LANES)] = summed
         mixed[place, pl.ds(LANES, LANES)] = turned
@@ -407,6 +414,10 @@
     out[...] = total * scaling
 
 
+def in_hbm(array):
+    return pltpu.with_memory_space_constraint(array, pltpu.HBM)
+
+
 def whole_call(kernel, out_shapes, scratch, operands, tables=(), kept=True):
     out_type = pltpu.VMEM if kept else jax.ShapeDtypeStruct
     operands = [pltpu.with_memory_space_constraint(operand, pltpu.VMEM) for operand in operands]
@@ -414,11 +425,11 @@
         kernel,
         out_shape=[out_type(shape, jnp.float32) for shape in out_shapes],
         in_specs=[pl.BlockSpec(memory_space=pltpu.VMEM)] * len(operands)
-        + [pl.BlockSpec(memory_space=pl.ANY)] * len(tables),
+        + [pl.BlockSpec(memory_space=pltpu.HBM)] * len(tables),
         out_specs=[pl.BlockSpec(memory_space=pltpu.VMEM)] * len(out_shapes),
         scratch_shapes=scratch,
         compiler_params=pltpu.CompilerParams(vmem_limit_bytes=VMEM_BYTES),
-    )(*operands, *tables)
+    )(*operands, *[in_hbm(table) for table in tables])
 
 
 def row_scratch(blocks, rows, terms, width, tables):
@@ -462,7 +473,9 @@
         return tile
 
     lined = [along(mine, step) for step in range(1, lines)]
-    flipped_own = across(mine)
+    own_source = ((0, 0, 0, 0), None, 0, False)
+    own = spectra([density], [own_source])
+    flipped_own = after(across(mine), own)
     line_near = jnp.stack(lined)
     near = jnp.concatenate([flipped_own[None], line_near])
     flipped_near = across(line_near)
@@ -471,19 +484,16 @@
     flipped_beyond = swapped(flipped_near, 2)
     flipped_beside = swapped(flipped_near, 1)
 
-    quarters = (1, 2, 3, 4)
-    early = [((0, 0, 0, 0), None, 0, False), (quarters, 0, 0, True)]
+    quarters = (0, 1, 2, 3)
+    early = [(quarters, 0, 0, True)]
     early += [(quarters, step, step, False) for step in range(1, lines)]
-    late = early[comps // 2 :]
-    early = early[: comps // 2]
-    first = spectra([density, *ready], early)
+    late = [(quarters, step - 1, step, True) for step in range(1, lines)]
+    first = spectra(ready, early)
     flipped_beyond = after(flipped_beyond, first)
     flipped = [flipped_near, flipped_beyond, flipped_beside, swapped(flipped_beyond, 1)]
-    late = [((0, 1, 2, 3), *rest) for _, *rest in late]
-    late += [((4, 5, 6, 7), step - 1, step, True) for step in range(1, lines)]
-    second = spectra([*ready, *flipped], late)
-    layout = [source[2:] for source in early + late]
-    return [first[None], second[None]], layout
+    second = spectra(flipped, late)
+    layout = [source[2:] for source in [own_source] + early + late]
+    return [own[None], first[None], second[None]], layout
 
 
 def spectra_by_gather(density, blocks, groups, columns, row_factors, tables):
@@ -501,11 +511,11 @@
         out_shape=jax.ShapeDtypeStruct((total_rows // 8, *tile_shape), jnp.float32),
         in_specs=[pl.BlockSpec((8 // rows_here, ranks, rows_here, part), lambda t: (t, 0, 0, 0))]
         + [pl.BlockSpec(memory_space=pltpu.VMEM)] * 4
-        + [pl.BlockSpec(memory_space=pl.ANY)] * len(tables),
+        + [pl.BlockSpec(memory_space=pltpu.HBM)] * len(tables),
         out_specs=pl.BlockSpec((1, *tile_shape), lambda t: (t, 0, 0, 0, 0, 0)),
         scratch_shapes=row_scratch(blocks, 8, terms, width, tables),
         compiler_params=pltpu.CompilerParams(vmem_limit_bytes=VMEM_BYTES),
-    )(gathered, *columns, *row_factors, *tables)
+    )(gathered, *columns, *row_factors, *[in_hbm(table) for table in tables])
     return [spectra], None
 
 
@@ -531,8 +541,9 @@
     tiles, layout = spectra(density, blocks, groups, columns, row_factors, tables)
 
     out_rows = total_rows * 2 * blocks
+    by_rank = total_rows == devices and 2 * blocks == 8
     (sent,) = whole_call(
-        lambda *refs: convolve_kernel(blocks, rows_here, layout, len(tiles), *refs),
+        lambda *refs: convolve_kernel(blocks, rows_here, layout, by_rank, len(tiles), *refs),
         [(out_rows, LANES)],
         [
             pltpu.VMEM((2 * blocks, 3, PAD + total_rows, terms, LANES), jnp.float32),
@@ -541,7 +552,13 @@
         ],
         (*tiles, split_rows(inverse_table())),
     )
-    spread = lax.all_to_all(sent, AXES, split_axis=0, concat_axis=0, tiled=True)
+    if by_rank:
+        ranks = devices // comps
+        spread = lax.all_to_all(sent, "rank", split_axis=0, concat_axis=0, tiled=True)
+        spread = spread.reshape(ranks, comps, 8, LANES).swapaxes(0, 1).reshape(out_rows, LANES)
+        spread = lax.all_to_all(spread, "comp", split_axis=0, concat_axis=0, tiled=True)
+    else:
+        spread = lax.all_to_all(sent, AXES, split_axis=0, concat_axis=0, tiled=True)
     inner_cos, inner_sin, outer_table = final_tables(devices, groups, blocks, width)
     scaling = 0.5 / (math.sqrt(total_rows * width) * width)
     (result,) = whole_call(

time: 53 us -> 56 us (1.057)
  blocking collectives: 11.5 us -> 17 us
  waiting for transfers between devices: 10 us -> 6.33 us
  Pallas kernels: 12.7 us -> 15.7 us
  local copies, waits for them, and re-layouts: 5.33 us -> 3.96 us
    all_to_all x1 -> x2, blocking collectives: 11.5 us -> 17 us  [the longest x1 9.87 us: body(): lax.all_to_all(spread, 'comp', split_axis=0, concat_axis=0, tiled=True)]
    ppermute x3, waiting for transfers between devices: 3.94 us -> 0.01 us  [along(): return lax.ppermute(block, 'comp', pairs)]
    pallas_call x4 -> x5, Pallas kernels: 12.7 us -> 15.7 us  [whole_call(): pl.pallas_call(kernel, out_shape=[out_type(shape, jnp.float32) for shape...]
    unnamed x30 -> x22, local copies, waits for them, and re-layouts: 4.4 us -> 3.08 us
  transfers between devices with their start and end apart: 11 -> 11, of which waited for: 3 -> 3; matrix products, arithmetic and copies ran while one was open for 0% -> 0% of each run, Pallas kernels for 8% -> 14%
where the time goes in v1:
time: 56 us; the launch traced here: 55.6 us
  blocking collectives  17 us (30%)
  Pallas kernels  15.7 us (28%)
  starting transfers between devices  12.3 us (22%)
  waiting for transfers between devices  6.33 us (11%)
  local copies, waits for them, and re-layouts  3.96 us (7%)
    pallas_call x5, Pallas kernels, whole_call(): pl.pallas_call(kernel, out_shape=[out_type(shape, jnp.float32) for shape...  15.7 us
    all_to_all x1, blocking collectives, body(): lax.all_to_all(spread, 'comp', split_axis=0, concat_axis=0, tiled=True)  9.87 us
    all_to_all x1, blocking collectives, body(): lax.all_to_all(sent, 'rank', split_axis=0, concat_axis=0, tiled=True)  7.15 us
    ppermute x6, waiting for transfers between devices, swapped(): return lax.ppermute(block, 'rank', [(r, r ^ other) for r in range(ranks)])  5.97 us
    ppermute x3, starting transfers between devices, along(): return lax.ppermute(block, 'comp', pairs)  5.51 us
    ppermute x2, starting transfers between devices, across(): return lax.ppermute(block, 'comp', [(c, c ^ 1) for c in range(comps)])  3.54 us
    ppermute x6, starting transfers between devices, swapped(): return lax.ppermute(block, 'rank', [(r, r ^ other) for r in range(ranks)])  3.29 us
    unnamed x22, local copies, waits for them, and re-layouts  3.08 us
  transfers between devices with their start and end apart: 11, of which 3 were waited for; matrix products, arithmetic and copies ran while one was open for 0% of the time, Pallas kernels for 14%

profile of v1, /device:TPU:0, one launch (start us, length us, event | category | flops | bytes accessed | tf_op | source)
XLA Modules:
  0.0 55.6 jit_solution(16089873962493354982)
XLA Ops:
  0.0 0.9 %constant_dynamic-slice_fusion = f32[4,4096]{1,0:T(4,128)S(1)} fusion(f32[4,16384]{1,0:T(4,128)} %refs_0_.1, s32[]{:T(128)S(6)} %select_n.3), kind=kLoop, calls=%fused_computation.3 | loop fusion | bytes 131076 | tf_op jit(solution)/shard_map/dynamic_slice | solution.py:452
  0.9 3.0 %collective-permute-start = (f32[4,4096]{1,0:T(4,128)S(1)}, f32[4,4096]{1,0:T(4,128)S(1)}, u32[]{:S(2)}, u32[]{:S(2)}) collective-permute-start(f32[4,4096]{1,0:T(4,128)S(1)} %constant_dynamic-slice_fusion), channel_id=1, source_target_pairs={{0,4},{4,0},{8,12},{12,8},{16,20},{20,16},{24,28},{28,24},{1,5},{5... | collective-permute-start | bytes 196616 | tf_op jit(solution)/shard_map/ppermute | solution.py:459
  3.8 1.6 %collective-permute-start.1 = (f32[4,4096]{1,0:T(4,128)S(1)}, f32[4,4096]{1,0:T(4,128)S(1)}, u32[]{:S(2)}, u32[]{:S(2)}) collective-permute-start(f32[4,4096]{1,0:T(4,128)S(1)} %constant_dynamic-slice_fusion), channel_id=1, source_target_pairs={{0,8},{4,12},{8,16},{12,20},{16,24},{20,28},{24,0},{28,4},{1,9},{5... | collective-permute-start | bytes 196616 | tf_op jit(solution)/shard_map/ppermute | solution.py:456
  5.4 2.6 %collective-permute-start.2 = (f32[4,4096]{1,0:T(4,128)S(1)}, f32[4,4096]{1,0:T(4,128)S(1)}, u32[]{:S(2)}, u32[]{:S(2)}) collective-permute-start(f32[4,4096]{1,0:T(4,128)S(1)} %constant_dynamic-slice_fusion), channel_id=1, source_target_pairs={{0,16},{4,20},{8,24},{12,28},{16,0},{20,4},{24,8},{28,12},{1,17},{... | collective-permute-start | bytes 196616 | tf_op jit(solution)/shard_map/ppermute | solution.py:456
  8.0 1.3 %collective-permute-start.3 = (f32[4,4096]{1,0:T(4,128)S(1)}, f32[4,4096]{1,0:T(4,128)S(1)}, u32[]{:S(2)}, u32[]{:S(2)}) collective-permute-start(f32[4,4096]{1,0:T(4,128)S(1)} %constant_dynamic-slice_fusion), channel_id=1, source_target_pairs={{0,24},{4,28},{8,0},{12,4},{16,8},{20,12},{24,16},{28,20},{1,25},{... | collective-permute-start | bytes 196616 | tf_op jit(solution)/shard_map/ppermute | solution.py:456
  9.4 0.0 copy-done.9
  9.4 0.0 copy-done.10
  9.4 1.0 %copy-done = f32[8,16384]{1,0:T(8,128)S(1)} copy-done((f32[8,16384]{1,0:T(8,128)S(1)}, f32[8,16384]{1,0:T(8,128)}, u32[]{:S(2)}) %copy-start) | copy-done | bytes 524312
  10.4 1.0 %copy-done.2 = f32[8,16384]{1,0:T(8,128)S(1)} copy-done((f32[8,16384]{1,0:T(8,128)S(1)}, f32[8,16384]{1,0:T(8,128)}, u32[]{:S(2)}) %copy-start.2) | copy-done | bytes 524312
  11.5 0.9 %copy-done.4 = f32[4,16384]{1,0:T(4,128)S(1)} copy-done((f32[4,16384]{1,0:T(4,128)S(1)}, f32[4,16384]{1,0:T(4,128)}, u32[]{:S(2)}) %copy-start.4) | copy-done | bytes 262168
  12.4 1.9 %shard_map.109.earlier = f32[8,2,4,8,128]{4,3,2,1,0:T(8,128)S(1)} custom-call(f32[4,16384]{1,0:T(4,128)S(1)} %copy-done.4, f32[8,16384]{1,0:T(8,128)S(1)} %copy-done, f32[8,16384]{1,0:T(8,128)S(1)} %copy-done.2, f32[8,32]{1,0:T(8,128)S(1)} %copy-done.9, f32[8,32]{1,0:T(8,128)S(1)} %copy-done.10, f32[4,2,8,128]{3,2,1,0:T(8,128)} %constant.22.clone.refs_5_.refs_8_, ...), custom_call_target="tpu_custom_call" | custom-call | tf_op jit(solution)/shard_map/pallas_call | solution.py:424
  14.3 0.0 collective-permute-done.value
  14.3 0.0 copy-start.3
  14.3 0.0 copy-start.1
  14.3 0.0 collective-permute-done.1
  14.3 0.0 collective-permute-done.2
  14.3 0.0 collective-permute-done.3
  14.4 0.1 pad_maximum_fusion.refs_0_
  14.4 1.6 %collective-permute-start.4 = (f32[4,4,4096]{2,1,0:T(4,128)S(1)}, f32[4,4,4096]{2,1,0:T(4,128)S(1)}, u32[]{:S(2)}, u32[]{:S(2)}) collective-permute-start(f32[4,4,4096]{2,1,0:T(4,128)S(1)} %pad_maximum_fusion.refs_0_), channel_id=1, source_target_pairs={{0,2},{1,3},{2,0},{3,1},{4,6},{5,7},{6,4},{7,5},{8,10},{9,11},{10,... | collective-permute-start | bytes 786440 | tf_op jit(solution)/shard_map/ppermute | solution.py:462
  16.0 0.6 %collective-permute-start.7 = (f32[3,4,4096]{2,1,0:T(4,128)S(1)}, f32[3,4,4096]{2,1,0:T(4,128)S(1)}, u32[]{:S(2)}, u32[]{:S(2)}) collective-permute-start(f32[3,4,4096]{2,1,0:T(4,128)S(1)} %pad_maximum_fusion.1), channel_id=1, source_target_pairs={{0,4},{4,0},{8,12},{12,8},{16,20},{20,16},{24,28},{28,24},{1,5},{5... | collective-permute-start | bytes 589832 | tf_op jit(solution)/shard_map/ppermute | solution.py:459
  16.6 0.0 collective-permute-start.5
  16.6 4.8 %collective-permute-done.4.refs_1_ = f32[4,4,4096]{2,1,0:T(4,128)S(1)} collective-permute-done((f32[4,4,4096]{2,1,0:T(4,128)S(1)}, f32[4,4,4096]{2,1,0:T(4,128)S(1)}, u32[]{:S(2)}, u32[]{:S(2)}) %collective-permute-start.4) | collective-permute-done | bytes 262176 | tf_op jit(solution)/shard_map/ppermute | solution.py:462
  21.4 0.0 collective-permute-start.6
  21.4 0.3 collective-permute-done.7.refs_0_
  21.8 1.2 %collective-permute-start.8 = (f32[3,4,4096]{2,1,0:T(4,128)S(1)}, f32[3,4,4096]{2,1,0:T(4,128)S(1)}, u32[]{:S(2)}, u32[]{:S(2)}) collective-permute-start(f32[3,4,4096]{2,1,0:T(4,128)S(1)} %collective-permute-done.7.refs_0_), channel_id=1, source_target_pairs={{0,2},{1,3},{2,0},{3,1},{4,6},{5,7},{6,4},{7,5},{8,10},{9,11},{10,... | collective-permute-start | bytes 589832 | tf_op jit(solution)/shard_map/ppermute | solution.py:462
  22.9 0.2 collective-permute-start.9
  23.1 0.0 collective-permute-done.5.refs_2_
  23.1 0.0 collective-permute-done.6.refs_3_
  23.1 0.0 copy-done.3
  23.2 0.0 copy-done.1
  23.2 5.9 %shard_map.111.earlier = f32[8,2,16,8,128]{4,3,2,1,0:T(8,128)S(1)} custom-call(f32[4,4,4096]{2,1,0:T(4,128)S(1)} %pad_maximum_fusion.refs_0_, f32[4,4,4096]{2,1,0:T(4,128)S(1)} %collective-permute-done.4.refs_1_, f32[4,4,4096]{2,1,0:T(4,128)S(1)} %collective-permute-done.5.refs_2_, f32[4,4,4096]{2,1,0:T(4,128)S(1)} %collective-permute-done.6.refs_3_, ...), custom_call_target="tpu_custom_call" | custom-call | tf_op jit(solution)/shard_map/pallas_call | solution.py:424
  29.1 0.0 collective-permute-done.8.value
  29.1 0.0 copy-start.6
  29.1 0.3 collective-permute-start.10
  29.5 0.0 collective-permute-done.9.refs_2_
  29.5 1.2 %collective-permute-done.10.refs_3_ = f32[3,4,4096]{2,1,0:T(4,128)S(1)} collective-permute-done((f32[3,4,4096]{2,1,0:T(4,128)S(1)}, f32[3,4,4096]{2,1,0:T(4,128)S(1)}, u32[]{:S(2)}, u32[]{:S(2)}) %collective-permute-start.10) | collective-permute-done | bytes 196640 | tf_op jit(solution)/shard_map/ppermute | solution.py:462
  30.6 4.1 %shard_map.113 = f32[8,2,12,8,128]{4,3,2,1,0:T(8,128)S(1)} custom-call(f32[3,4,4096]{2,1,0:T(4,128)S(1)} %collective-permute-done.7.refs_0_, f32[3,4,4096]{2,1,0:T(4,128)S(1)} %shard_map.112.refs_1_, f32[3,4,4096]{2,1,0:T(4,128)S(1)} %collective-permute-done.9.refs_2_, f32[3,4,4096]{2,1,0:T(4,128)S(1)} %collective-permute-done.10.refs_3_, ...), custom_call_target="tpu_custom_call" | custom-call | tf_op jit(solution)/shard_map/pallas_call | solution.py:424
  34.7 0.0 copy-done.6
  34.7 2.9 %shard_map.114 = f32[256,128]{1,0:T(8,128)S(1)} custom-call(f32[1,8,2,4,8,128]{5,4,3,2,1,0:T(8,128)S(1)} %bitcast.19, f32[1,8,2,16,8,128]{5,4,3,2,1,0:T(8,128)S(1)} %bitcast.17, f32[1,8,2,12,8,128]{5,4,3,2,1,0:T(8,128)S(1)} %bitcast.18, bf16[768,128]{1,0:T(8,128)(2,1)S(1)} %copy-done.6), custom_call_target="tpu_custom_call" | custom-call | tf_op jit(solution)/shard_map/pallas_call | solution.py:424
  37.6 0.0 copy-start.5
  37.6 7.2 %all_to_all.20 = f32[4,64,128]{2,1,0:T(8,128)S(1)} all-to-all(f32[4,64,128]{2,1,0:T(8,128)S(1)} %bitcast.20), channel_id=1, replica_groups=mesh['comp'=8,'rank'=4] {'rank'}, dimensions={0} | all-to-all | bytes 262144 | tf_op jit(solution)/shard_map/all_to_all | solution.py:557
  44.8 0.0 copy-start.7
  44.8 0.0 copy-start.8
  44.8 9.9 %all_to_all.21 = f32[8,32,128]{2,1,0:T(8,128)S(1)} all-to-all(f32[8,32,128]{2,1,0:T(8,128)S(1)} %copy_bitcast_fusion), channel_id=1, replica_groups=mesh['comp'=8,'rank'=4] {'comp'}, dimensions={0} | all-to-all | bytes 262144 | tf_op jit(solution)/shard_map/all_to_all | solution.py:559
  54.7 0.0 copy-done.5
  54.7 0.0 copy-done.7
  54.7 0.0 copy-done.8
  54.7 0.9 %shard_map.115 = f32[128,128]{1,0:T(8,128)} custom-call(f32[256,128]{1,0:T(8,128)S(1)} %bitcast.21, f32[256,128]{1,0:T(8,128)S(1)} %copy-done.7, f32[256,128]{1,0:T(8,128)S(1)} %copy-done.8, bf16[128,1536]{1,0:T(8,128)(2,1)S(1)} %copy-done.5), custom_call_target="tpu_custom_call" | custom-call | tf_op jit(solution)/shard_map/pallas_call | solution.py:424
  (9 shorter events, 0.1 us)
Async XLA Ops:
  0.0 9.4 %copy-start.9 = (f32[8,32]{1,0:T(8,128)S(1)}, f32[8,32]{1,0:T(8,128)}, u32[]{:S(2)}) copy-start(f32[8,32]{1,0:T(8,128)} %refs_6_.3) | copy-start | bytes 3076
  0.0 9.4 %copy-start.10 = (f32[8,32]{1,0:T(8,128)S(1)}, f32[8,32]{1,0:T(8,128)}, u32[]{:S(2)}) copy-start(f32[8,32]{1,0:T(8,128)} %refs_7_.3) | copy-start | bytes 3076
  0.9 13.4 %collective-permute-start = (f32[4,4096]{1,0:T(4,128)S(1)}, f32[4,4096]{1,0:T(4,128)S(1)}, u32[]{:S(2)}, u32[]{:S(2)}) collective-permute-start(f32[4,4096]{1,0:T(4,128)S(1)} %constant_dynamic-slice_fusion), channel_id=1, source_target_pairs={{0,4},{4,0},{8,12},{12,8},{16,20},{20,16},{24,28},{28,24},{1,5},{5... | collective-permute-start | bytes 196616 | tf_op jit(solution)/shard_map/ppermute | solution.py:459
  3.8 10.5 %collective-permute-start.1 = (f32[4,4096]{1,0:T(4,128)S(1)}, f32[4,4096]{1,0:T(4,128)S(1)}, u32[]{:S(2)}, u32[]{:S(2)}) collective-permute-start(f32[4,4096]{1,0:T(4,128)S(1)} %constant_dynamic-slice_fusion), channel_id=1, source_target_pairs={{0,8},{4,12},{8,16},{12,20},{16,24},{20,28},{24,0},{28,4},{1,9},{5... | collective-permute-start | bytes 196616 | tf_op jit(solution)/shard_map/ppermute | solution.py:456
  5.4 8.9 %collective-permute-start.2 = (f32[4,4096]{1,0:T(4,128)S(1)}, f32[4,4096]{1,0:T(4,128)S(1)}, u32[]{:S(2)}, u32[]{:S(2)}) collective-permute-start(f32[4,4096]{1,0:T(4,128)S(1)} %constant_dynamic-slice_fusion), channel_id=1, source_target_pairs={{0,16},{4,20},{8,24},{12,28},{16,0},{20,4},{24,8},{28,12},{1,17},{... | collective-permute-start | bytes 196616 | tf_op jit(solution)/shard_map/ppermute | solution.py:456
  8.0 6.3 %collective-permute-start.3 = (f32[4,4096]{1,0:T(4,128)S(1)}, f32[4,4096]{1,0:T(4,128)S(1)}, u32[]{:S(2)}, u32[]{:S(2)}) collective-permute-start(f32[4,4096]{1,0:T(4,128)S(1)} %constant_dynamic-slice_fusion), channel_id=1, source_target_pairs={{0,24},{4,28},{8,0},{12,4},{16,8},{20,12},{24,16},{28,20},{1,25},{... | collective-permute-start | bytes 196616 | tf_op jit(solution)/shard_map/ppermute | solution.py:456
  9.4 1.0 %copy-start = (f32[8,16384]{1,0:T(8,128)S(1)}, f32[8,16384]{1,0:T(8,128)}, u32[]{:S(2)}) copy-start(f32[8,16384]{1,0:T(8,128)} %refs_4_.5) | copy-start | bytes 1572868
  10.4 1.0 %copy-start.2 = (f32[8,16384]{1,0:T(8,128)S(1)}, f32[8,16384]{1,0:T(8,128)}, u32[]{:S(2)}) copy-start(f32[8,16384]{1,0:T(8,128)} %refs_5_.4) | copy-start | bytes 1572868
  11.4 0.9 %copy-start.4 = (f32[4,16384]{1,0:T(4,128)S(1)}, f32[4,16384]{1,0:T(4,128)}, u32[]{:S(2)}) copy-start(f32[4,16384]{1,0:T(4,128)} %refs_0_.1) | copy-start | bytes 786436
  14.3 8.9 %copy-start.3 = (f32[8,16384]{1,0:T(8,128)S(1)}, f32[8,16384]{1,0:T(8,128)}, u32[]{:S(2)}) copy-start(f32[8,16384]{1,0:T(8,128)} %refs_5_.4) | copy-start | bytes 1572868
  14.3 8.8 %copy-start.1 = (f32[8,16384]{1,0:T(8,128)S(1)}, f32[8,16384]{1,0:T(8,128)}, u32[]{:S(2)}) copy-start(f32[8,16384]{1,0:T(8,128)} %refs_4_.5) | copy-start | bytes 1572868
  14.4 7.0 %collective-permute-start.4 = (f32[4,4,4096]{2,1,0:T(4,128)S(1)}, f32[4,4,4096]{2,1,0:T(4,128)S(1)}, u32[]{:S(2)}, u32[]{:S(2)}) collective-permute-start(f32[4,4,4096]{2,1,0:T(4,128)S(1)} %pad_maximum_fusion.refs_0_), channel_id=1, source_target_pairs={{0,2},{1,3},{2,0},{3,1},{4,6},{5,7},{6,4},{7,5},{8,10},{9,11},{10,... | collective-permute-start | bytes 786440 | tf_op jit(solution)/shard_map/ppermute | solution.py:462
  16.0 5.7 %collective-permute-start.7 = (f32[3,4,4096]{2,1,0:T(4,128)S(1)}, f32[3,4,4096]{2,1,0:T(4,128)S(1)}, u32[]{:S(2)}, u32[]{:S(2)}) collective-permute-start(f32[3,4,4096]{2,1,0:T(4,128)S(1)} %pad_maximum_fusion.1), channel_id=1, source_target_pairs={{0,4},{4,0},{8,12},{12,8},{16,20},{20,16},{24,28},{28,24},{1,5},{5... | collective-permute-start | bytes 589832 | tf_op jit(solution)/shard_map/ppermute | solution.py:459
  16.6 6.5 %collective-permute-start.5 = (f32[4,4,4096]{2,1,0:T(4,128)S(1)}, f32[4,4,4096]{2,1,0:T(4,128)S(1)}, u32[]{:S(2)}, u32[]{:S(2)}) collective-permute-start(f32[4,4,4096]{2,1,0:T(4,128)S(1)} %pad_maximum_fusion.refs_0_), channel_id=1, source_target_pairs={{0,1},{1,0},{2,3},{3,2},{4,5},{5,4},{6,7},{7,6},{8,9},{9,8},{10,11... | collective-permute-start | bytes 786440 | tf_op jit(solution)/shard_map/ppermute | solution.py:462
  21.4 1.7 %collective-permute-start.6 = (f32[4,4,4096]{2,1,0:T(4,128)S(1)}, f32[4,4,4096]{2,1,0:T(4,128)S(1)}, u32[]{:S(2)}, u32[]{:S(2)}) collective-permute-start(f32[4,4,4096]{2,1,0:T(4,128)S(1)} %collective-permute-done.4.refs_1_), channel_id=1, source_target_pairs={{0,1},{1,0},{2,3},{3,2},{4,5},{5,4},{6,7},{7,6},{8,9},{9,8},{10,11... | collective-permute-start | bytes 786440 | tf_op jit(solution)/shard_map/ppermute | solution.py:462
  21.8 7.3 %collective-permute-start.8 = (f32[3,4,4096]{2,1,0:T(4,128)S(1)}, f32[3,4,4096]{2,1,0:T(4,128)S(1)}, u32[]{:S(2)}, u32[]{:S(2)}) collective-permute-start(f32[3,4,4096]{2,1,0:T(4,128)S(1)} %collective-permute-done.7.refs_0_), channel_id=1, source_target_pairs={{0,2},{1,3},{2,0},{3,1},{4,6},{5,7},{6,4},{7,5},{8,10},{9,11},{10,... | collective-permute-start | bytes 589832 | tf_op jit(solution)/shard_map/ppermute | solution.py:462
  22.9 6.5 %collective-permute-start.9 = (f32[3,4,4096]{2,1,0:T(4,128)S(1)}, f32[3,4,4096]{2,1,0:T(4,128)S(1)}, u32[]{:S(2)}, u32[]{:S(2)}) collective-permute-start(f32[3,4,4096]{2,1,0:T(4,128)S(1)} %collective-permute-done.7.refs_0_), channel_id=1, source_target_pairs={{0,1},{1,0},{2,3},{3,2},{4,5},{5,4},{6,7},{7,6},{8,9},{9,8},{10,11... | collective-permute-start | bytes 589832 | tf_op jit(solution)/shard_map/ppermute | solution.py:462
  29.1 5.6 %copy-start.6 = (bf16[768,128]{1,0:T(8,128)(2,1)S(1)}, bf16[768,128]{1,0:T(8,128)(2,1)}, u32[]{:S(2)}) copy-start(bf16[768,128]{1,0:T(8,128)(2,1)} %constant.38.refs_3_) | copy-start | bytes 589828
  29.1 1.5 %collective-permute-start.10 = (f32[3,4,4096]{2,1,0:T(4,128)S(1)}, f32[3,4,4096]{2,1,0:T(4,128)S(1)}, u32[]{:S(2)}, u32[]{:S(2)}) collective-permute-start(f32[3,4,4096]{2,1,0:T(4,128)S(1)} %shard_map.112.refs_1_), channel_id=1, source_target_pairs={{0,1},{1,0},{2,3},{3,2},{4,5},{5,4},{6,7},{7,6},{8,9},{9,8},{10,11... | collective-permute-start | bytes 589832 | tf_op jit(solution)/shard_map/ppermute | solution.py:462
  37.6 17.1 %copy-start.5 = (bf16[128,1536]{1,0:T(8,128)(2,1)S(1)}, bf16[128,1536]{1,0:T(8,128)(2,1)}, u32[]{:S(2)}) copy-start(bf16[128,1536]{1,0:T(8,128)(2,1)} %constant.43.refs_3_) | copy-start | bytes 1179652
  44.8 9.9 %copy-start.7 = (f32[256,128]{1,0:T(8,128)S(1)}, f32[256,128]{1,0:T(8,128)}, u32[]{:S(2)}) copy-start(f32[256,128]{1,0:T(8,128)} %constant.25.clone.refs_1_) | copy-start | bytes 393220
  44.8 9.9 %copy-start.8 = (f32[256,128]{1,0:T(8,128)S(1)}, f32[256,128]{1,0:T(8,128)}, u32[]{:S(2)}) copy-start(f32[256,128]{1,0:T(8,128)} %constant.26.clone.refs_2_) | copy-start | bytes 393220

commit v2 on v1

--- a/solution.py
+++ b/solution.py
@@ -119,13 +119,12 @@
             for k in range(4):
                 partial[k, block, first + row] = sums[row * 4 + k]
 
-    for first in range(0, rows, 8):
-
-        def reduce_tile(block, carry, first=first):
+    def reduce_tiles(block, carry):
+        for first in range(0, rows, 8):
             reduce_block(block, first, min(8, rows - first))
-            return carry
-
-        lax.fori_loop(0, blocks, reduce_tile, 0)
+        return carry
+
+    lax.fori_loop(0, blocks, reduce_tiles, 0)
 
 
 def transform_rows(blocks, rows, row_at, row_factors, twiddle, table, out, partial, joined):
@@ -310,7 +309,7 @@
     )(*[pltpu.with_memory_space_constraint(array, pltpu.VMEM) for array in (value, earlier)])
 
 
-def convolve_kernel(blocks, rows_here, layout, by_rank, tile_count, *refs):
+def convolve_kernel(blocks, rows_here, layout, tile_count, *refs):
     tiles = refs[:tile_count]
     back, out, spectrum, product, mixed = refs[tile_count:]
     total_rows = spectrum.shape[2] - PAD
@@ -393,9 +392,6 @@
                 for k in range(8)
             ]
             turned = jnp.sum(jnp.stack(swapped), axis=1)
-        if by_rank:
-            ranks = lax.axis_size("rank")
-            at = lax.rem(at, ranks) * (total_rows // ranks) + lax.div(at, ranks)
         place = pl.ds(pl.multiple_of(at * 8, 8), 8)
         mixed[place, pl.ds(0, LANES)] = summed
         mixed[place, pl.ds(LANES, LANES)] = turned
@@ -541,9 +537,8 @@
     tiles, layout = spectra(density, blocks, groups, columns, row_factors, tables)
 
     out_rows = total_rows * 2 * blocks
-    by_rank = total_rows == devices and 2 * blocks == 8
     (sent,) = whole_call(
-        lambda *refs: convolve_kernel(blocks, rows_here, layout, by_rank, len(tiles), *refs),
+        lambda *refs: convolve_kernel(blocks, rows_here, layout, len(tiles), *refs),
         [(out_rows, LANES)],
         [
             pltpu.VMEM((2 * blocks, 3, PAD + total_rows, terms, LANES), jnp.float32),
@@ -552,13 +547,7 @@
         ],
         (*tiles, split_rows(inverse_table())),
     )
-    if by_rank:
-        ranks = devices // comps
-        spread = lax.all_to_all(sent, "rank", split_axis=0, concat_axis=0, tiled=True)
-        spread = spread.reshape(ranks, comps, 8, LANES).swapaxes(0, 1).reshape(out_rows, LANES)
-        spread = lax.all_to_all(spread, "comp", split_axis=0, concat_axis=0, tiled=True)
-    else:
-        spread = lax.all_to_all(sent, AXES, split_axis=0, concat_axis=0, tiled=True)
+    spread = lax.all_to_all(sent, AXES, split_axis=0, concat_axis=0, tiled=True)
     inner_cos, inner_sin, outer_table = final_tables(devices, groups, blocks, width)
     scaling = 0.5 / (math.sqrt(total_rows * width) * width)
     (result,) = whole_call(

time: 56 us -> 47.4 us (0.85)
  blocking collectives: 17 us -> 10.1 us
  Pallas kernels: 15.7 us -> 12.4 us
  waiting for transfers between devices: 6.33 us -> 8.4 us
    all_to_all x2 -> x1, blocking collectives: 17 us -> 10.1 us  [body(): spread = lax.all_to_all(sent, AXES, split_axis=0, concat_axis=0, tiled=True)]
    pallas_call x5, Pallas kernels: 15.7 us -> 12.4 us  [whole_call(): pl.pallas_call(kernel, out_shape=[out_type(shape, jnp.float32) for shape...]
    ppermute x6, waiting for transfers between devices: 5.97 us -> 8.05 us  [swapped(): return lax.ppermute(block, 'rank', [(r, r ^ other) for r in range(ranks)])]
  transfers between devices with their start and end apart: 11 -> 11, of which waited for: 3 -> 4; matrix products, arithmetic and copies ran while one was open for 0% -> 0% of each run, Pallas kernels for 14% -> 12%
where the time goes in v2:
time: 47.4 us; the launch traced here: 47.1 us
  Pallas kernels  12.4 us (26%)
  starting transfers between devices  12 us (25%)
  blocking collectives  10.1 us (21%)
  waiting for transfers between devices  8.4 us (18%)
  local copies, waits for them, and re-layouts  3.95 us (8%)
    pallas_call x5, Pallas kernels, whole_call(): pl.pallas_call(kernel, out_shape=[out_type(shape, jnp.float32) for shape...  12.4 us
    all_to_all x1, blocking collectives, body(): spread = lax.all_to_all(sent, AXES, split_axis=0, concat_axis=0, tiled=True)  10.1 us
    ppermute x6, waiting for transfers between devices, swapped(): return lax.ppermute(block, 'rank', [(r, r ^ other) for r in range(ranks)])  8.05 us
    ppermute x3, starting transfers between devices, along(): return lax.ppermute(block, 'comp', pairs)  5.51 us
    ppermute x2, starting transfers between devices, across(): return lax.ppermute(block, 'comp', [(c, c ^ 1) for c in range(comps)])  3.54 us
    unnamed x22, local copies, waits for them, and re-layouts  3.08 us
    ppermute x6, starting transfers between devices, swapped(): return lax.ppermute(block, 'rank', [(r, r ^ other) for r in range(ranks)])  2.94 us
  transfers between devices with their start and end apart: 11, of which 4 were waited for; matrix products, arithmetic and copies ran while one was open for 0% of the time, Pallas kernels for 12%

profile of v2, /device:TPU:0, one launch (start us, length us, event | category | flops | bytes accessed | tf_op | source)
XLA Modules:
  0.0 47.1 jit_solution(1993910532649943747)
XLA Ops:
  0.0 0.0 copy-start.10
  0.0 0.9 %constant_dynamic-slice_fusion = f32[4,4096]{1,0:T(4,128)S(1)} fusion(f32[4,16384]{1,0:T(4,128)} %refs_0_.1, s32[]{:T(128)S(6)} %select_n.3), kind=kLoop, calls=%fused_computation.2 | loop fusion | bytes 131076 | tf_op jit(solution)/shard_map/dynamic_slice | solution.py:448
  0.9 3.0 %collective-permute-start = (f32[4,4096]{1,0:T(4,128)S(1)}, f32[4,4096]{1,0:T(4,128)S(1)}, u32[]{:S(2)}, u32[]{:S(2)}) collective-permute-start(f32[4,4096]{1,0:T(4,128)S(1)} %constant_dynamic-slice_fusion), channel_id=1, source_target_pairs={{0,4},{4,0},{8,12},{12,8},{16,20},{20,16},{24,28},{28,24},{1,5},{5... | collective-permute-start | bytes 196616 | tf_op jit(solution)/shard_map/ppermute | solution.py:455
  3.8 1.6 %collective-permute-start.1 = (f32[4,4096]{1,0:T(4,128)S(1)}, f32[4,4096]{1,0:T(4,128)S(1)}, u32[]{:S(2)}, u32[]{:S(2)}) collective-permute-start(f32[4,4096]{1,0:T(4,128)S(1)} %constant_dynamic-slice_fusion), channel_id=1, source_target_pairs={{0,8},{4,12},{8,16},{12,20},{16,24},{20,28},{24,0},{28,4},{1,9},{5... | collective-permute-start | bytes 196616 | tf_op jit(solution)/shard_map/ppermute | solution.py:452
  5.4 2.6 %collective-permute-start.2 = (f32[4,4096]{1,0:T(4,128)S(1)}, f32[4,4096]{1,0:T(4,128)S(1)}, u32[]{:S(2)}, u32[]{:S(2)}) collective-permute-start(f32[4,4096]{1,0:T(4,128)S(1)} %constant_dynamic-slice_fusion), channel_id=1, source_target_pairs={{0,16},{4,20},{8,24},{12,28},{16,0},{20,4},{24,8},{28,12},{1,17},{... | collective-permute-start | bytes 196616 | tf_op jit(solution)/shard_map/ppermute | solution.py:452
  8.0 1.3 %collective-permute-start.3 = (f32[4,4096]{1,0:T(4,128)S(1)}, f32[4,4096]{1,0:T(4,128)S(1)}, u32[]{:S(2)}, u32[]{:S(2)}) collective-permute-start(f32[4,4096]{1,0:T(4,128)S(1)} %constant_dynamic-slice_fusion), channel_id=1, source_target_pairs={{0,24},{4,28},{8,0},{12,4},{16,8},{20,12},{24,16},{28,20},{1,25},{... | collective-permute-start | bytes 196616 | tf_op jit(solution)/shard_map/ppermute | solution.py:452
  9.4 0.0 copy-done.9
  9.4 0.0 copy-done.10
  9.4 0.0 copy-start
  9.4 1.0 %copy-done = f32[8,16384]{1,0:T(8,128)S(1)} copy-done((f32[8,16384]{1,0:T(8,128)S(1)}, f32[8,16384]{1,0:T(8,128)}, u32[]{:S(2)}) %copy-start) | copy-done | bytes 524312
  10.4 1.0 %copy-done.2 = f32[8,16384]{1,0:T(8,128)S(1)} copy-done((f32[8,16384]{1,0:T(8,128)S(1)}, f32[8,16384]{1,0:T(8,128)}, u32[]{:S(2)}) %copy-start.2) | copy-done | bytes 524312
  11.5 0.9 %copy-done.4 = f32[4,16384]{1,0:T(4,128)S(1)} copy-done((f32[4,16384]{1,0:T(4,128)S(1)}, f32[4,16384]{1,0:T(4,128)}, u32[]{:S(2)}) %copy-start.4) | copy-done | bytes 262168
  12.4 1.9 %shard_map.109.earlier = f32[8,2,4,8,128]{4,3,2,1,0:T(8,128)S(1)} custom-call(f32[4,16384]{1,0:T(4,128)S(1)} %copy-done.4, f32[8,16384]{1,0:T(8,128)S(1)} %copy-done, f32[8,16384]{1,0:T(8,128)S(1)} %copy-done.2, f32[8,32]{1,0:T(8,128)S(1)} %copy-done.9, f32[8,32]{1,0:T(8,128)S(1)} %copy-done.10, f32[4,2,8,128]{3,2,1,0:T(8,128)} %constant.22.clone.refs_5_.refs_8_, ...), custom_call_target="tpu_custom_call" | custom-call | tf_op jit(solution)/shard_map/pallas_call | solution.py:420
  14.3 0.0 collective-permute-done.value
  14.3 0.0 copy-start.3
  14.3 0.0 copy-start.1
  14.3 0.0 collective-permute-done.1
  14.3 0.0 collective-permute-done.2
  14.3 0.0 collective-permute-done.3
  14.4 0.1 pad_maximum_fusion.refs_0_
  14.4 1.6 %collective-permute-start.4 = (f32[4,4,4096]{2,1,0:T(4,128)S(1)}, f32[4,4,4096]{2,1,0:T(4,128)S(1)}, u32[]{:S(2)}, u32[]{:S(2)}) collective-permute-start(f32[4,4,4096]{2,1,0:T(4,128)S(1)} %pad_maximum_fusion.refs_0_), channel_id=1, source_target_pairs={{0,2},{1,3},{2,0},{3,1},{4,6},{5,7},{6,4},{7,5},{8,10},{9,11},{10,... | collective-permute-start | bytes 786440 | tf_op jit(solution)/shard_map/ppermute | solution.py:458
  16.0 0.6 %collective-permute-start.7 = (f32[3,4,4096]{2,1,0:T(4,128)S(1)}, f32[3,4,4096]{2,1,0:T(4,128)S(1)}, u32[]{:S(2)}, u32[]{:S(2)}) collective-permute-start(f32[3,4,4096]{2,1,0:T(4,128)S(1)} %pad_maximum_fusion.1), channel_id=1, source_target_pairs={{0,4},{4,0},{8,12},{12,8},{16,20},{20,16},{24,28},{28,24},{1,5},{5... | collective-permute-start | bytes 589832 | tf_op jit(solution)/shard_map/ppermute | solution.py:455
  16.6 0.0 collective-permute-start.5
  16.6 4.8 %collective-permute-done.4.refs_1_ = f32[4,4,4096]{2,1,0:T(4,128)S(1)} collective-permute-done((f32[4,4,4096]{2,1,0:T(4,128)S(1)}, f32[4,4,4096]{2,1,0:T(4,128)S(1)}, u32[]{:S(2)}, u32[]{:S(2)}) %collective-permute-start.4) | collective-permute-done | bytes 262176 | tf_op jit(solution)/shard_map/ppermute | solution.py:458
  21.4 0.0 collective-permute-start.6
  21.4 0.3 collective-permute-done.7.refs_0_
  21.8 1.2 %collective-permute-start.8 = (f32[3,4,4096]{2,1,0:T(4,128)S(1)}, f32[3,4,4096]{2,1,0:T(4,128)S(1)}, u32[]{:S(2)}, u32[]{:S(2)}) collective-permute-start(f32[3,4,4096]{2,1,0:T(4,128)S(1)} %collective-permute-done.7.refs_0_), channel_id=1, source_target_pairs={{0,2},{1,3},{2,0},{3,1},{4,6},{5,7},{6,4},{7,5},{8,10},{9,11},{10,... | collective-permute-start | bytes 589832 | tf_op jit(solution)/shard_map/ppermute | solution.py:458
  22.9 0.2 collective-permute-start.9
  23.1 0.0 collective-permute-done.5.refs_2_
  23.1 0.0 collective-permute-done.6.refs_3_
  23.1 0.0 copy-done.3
  23.2 0.0 copy-done.1
  23.2 3.8 %shard_map.111.earlier = f32[8,2,16,8,128]{4,3,2,1,0:T(8,128)S(1)} custom-call(f32[4,4,4096]{2,1,0:T(4,128)S(1)} %pad_maximum_fusion.refs_0_, f32[4,4,4096]{2,1,0:T(4,128)S(1)} %collective-permute-done.4.refs_1_, f32[4,4,4096]{2,1,0:T(4,128)S(1)} %collective-permute-done.5.refs_2_, f32[4,4,4096]{2,1,0:T(4,128)S(1)} %collective-permute-done.6.refs_3_, ...), custom_call_target="tpu_custom_call" | custom-call | tf_op jit(solution)/shard_map/pallas_call | solution.py:420
  26.9 1.8 %collective-permute-done.8.value = f32[3,4,4096]{2,1,0:T(4,128)S(1)} collective-permute-done((f32[3,4,4096]{2,1,0:T(4,128)S(1)}, f32[3,4,4096]{2,1,0:T(4,128)S(1)}, u32[]{:S(2)}, u32[]{:S(2)}) %collective-permute-start.8) | collective-permute-done | bytes 196640 | tf_op jit(solution)/shard_map/ppermute | solution.py:458
  28.7 0.0 collective-permute-start.10
  28.7 0.0 collective-permute-done.9.refs_2_
  28.8 1.4 %collective-permute-done.10.refs_3_ = f32[3,4,4096]{2,1,0:T(4,128)S(1)} collective-permute-done((f32[3,4,4096]{2,1,0:T(4,128)S(1)}, f32[3,4,4096]{2,1,0:T(4,128)S(1)}, u32[]{:S(2)}, u32[]{:S(2)}) %collective-permute-start.10) | collective-permute-done | bytes 196640 | tf_op jit(solution)/shard_map/ppermute | solution.py:458
  30.2 3.0 %shard_map.113 = f32[8,2,12,8,128]{4,3,2,1,0:T(8,128)S(1)} custom-call(f32[3,4,4096]{2,1,0:T(4,128)S(1)} %collective-permute-done.7.refs_0_, f32[3,4,4096]{2,1,0:T(4,128)S(1)} %shard_map.112.refs_1_, f32[3,4,4096]{2,1,0:T(4,128)S(1)} %collective-permute-done.9.refs_2_, f32[3,4,4096]{2,1,0:T(4,128)S(1)} %collective-permute-done.10.refs_3_, ...), custom_call_target="tpu_custom_call" | custom-call | tf_op jit(solution)/shard_map/pallas_call | solution.py:420
  33.2 0.0 copy-done.6
  33.2 0.0 copy-start.5
  33.2 2.9 %shard_map.114 = f32[256,128]{1,0:T(8,128)S(1)} custom-call(f32[1,8,2,4,8,128]{5,4,3,2,1,0:T(8,128)S(1)} %bitcast.12, f32[1,8,2,16,8,128]{5,4,3,2,1,0:T(8,128)S(1)} %bitcast.10, f32[1,8,2,12,8,128]{5,4,3,2,1,0:T(8,128)S(1)} %bitcast.11, bf16[768,128]{1,0:T(8,128)(2,1)S(1)} %copy-done.6), custom_call_target="tpu_custom_call" | custom-call | tf_op jit(solution)/shard_map/pallas_call | solution.py:420
  36.1 0.0 copy-start.7
  36.1 0.0 copy-start.8
  36.1 10.1 %all_to_all.11 = f32[32,8,128]{2,1,0:T(8,128)S(1)} all-to-all(f32[32,8,128]{2,1,0:T(8,128)S(1)} %bitcast.13), channel_id=1, replica_groups=mesh['comp'=8,'rank'=4] {'comp','rank'}, dimensions={0} | all-to-all | bytes 262144 | tf_op jit(solution)/shard_map/all_to_all | solution.py:550
  46.2 0.0 copy-done.5
  46.2 0.0 copy-done.7
  46.2 0.0 copy-done.8
  46.2 0.9 %shard_map.115 = f32[128,128]{1,0:T(8,128)} custom-call(f32[256,128]{1,0:T(8,128)S(1)} %bitcast.14, f32[256,128]{1,0:T(8,128)S(1)} %copy-done.7, f32[256,128]{1,0:T(8,128)S(1)} %copy-done.8, bf16[128,1536]{1,0:T(8,128)(2,1)S(1)} %copy-done.5), custom_call_target="tpu_custom_call" | custom-call | tf_op jit(solution)/shard_map/pallas_call | solution.py:420
  (7 shorter events, 0.1 us)
Async XLA Ops:
  0.0 9.4 %copy-start.9 = (f32[8,32]{1,0:T(8,128)S(1)}, f32[8,32]{1,0:T(8,128)}, u32[]{:S(2)}) copy-start(f32[8,32]{1,0:T(8,128)} %refs_6_.3) | copy-start | bytes 3076
  0.0 9.4 %copy-start.10 = (f32[8,32]{1,0:T(8,128)S(1)}, f32[8,32]{1,0:T(8,128)}, u32[]{:S(2)}) copy-start(f32[8,32]{1,0:T(8,128)} %refs_7_.3) | copy-start | bytes 3076
  0.9 13.4 %collective-permute-start = (f32[4,4096]{1,0:T(4,128)S(1)}, f32[4,4096]{1,0:T(4,128)S(1)}, u32[]{:S(2)}, u32[]{:S(2)}) collective-permute-start(f32[4,4096]{1,0:T(4,128)S(1)} %constant_dynamic-slice_fusion), channel_id=1, source_target_pairs={{0,4},{4,0},{8,12},{12,8},{16,20},{20,16},{24,28},{28,24},{1,5},{5... | collective-permute-start | bytes 196616 | tf_op jit(solution)/shard_map/ppermute | solution.py:455
  3.8 10.5 %collective-permute-start.1 = (f32[4,4096]{1,0:T(4,128)S(1)}, f32[4,4096]{1,0:T(4,128)S(1)}, u32[]{:S(2)}, u32[]{:S(2)}) collective-permute-start(f32[4,4096]{1,0:T(4,128)S(1)} %constant_dynamic-slice_fusion), channel_id=1, source_target_pairs={{0,8},{4,12},{8,16},{12,20},{16,24},{20,28},{24,0},{28,4},{1,9},{5... | collective-permute-start | bytes 196616 | tf_op jit(solution)/shard_map/ppermute | solution.py:452
  5.4 8.9 %collective-permute-start.2 = (f32[4,4096]{1,0:T(4,128)S(1)}, f32[4,4096]{1,0:T(4,128)S(1)}, u32[]{:S(2)}, u32[]{:S(2)}) collective-permute-start(f32[4,4096]{1,0:T(4,128)S(1)} %constant_dynamic-slice_fusion), channel_id=1, source_target_pairs={{0,16},{4,20},{8,24},{12,28},{16,0},{20,4},{24,8},{28,12},{1,17},{... | collective-permute-start | bytes 196616 | tf_op jit(solution)/shard_map/ppermute | solution.py:452
  8.0 6.3 %collective-permute-start.3 = (f32[4,4096]{1,0:T(4,128)S(1)}, f32[4,4096]{1,0:T(4,128)S(1)}, u32[]{:S(2)}, u32[]{:S(2)}) collective-permute-start(f32[4,4096]{1,0:T(4,128)S(1)} %constant_dynamic-slice_fusion), channel_id=1, source_target_pairs={{0,24},{4,28},{8,0},{12,4},{16,8},{20,12},{24,16},{28,20},{1,25},{... | collective-permute-start | bytes 196616 | tf_op jit(solution)/shard_map/ppermute | solution.py:452
  9.4 1.0 %copy-start = (f32[8,16384]{1,0:T(8,128)S(1)}, f32[8,16384]{1,0:T(8,128)}, u32[]{:S(2)}) copy-start(f32[8,16384]{1,0:T(8,128)} %refs_4_.5) | copy-start | bytes 1572868
  10.4 1.0 %copy-start.2 = (f32[8,16384]{1,0:T(8,128)S(1)}, f32[8,16384]{1,0:T(8,128)}, u32[]{:S(2)}) copy-start(f32[8,16384]{1,0:T(8,128)} %refs_5_.4) | copy-start | bytes 1572868
  11.4 0.9 %copy-start.4 = (f32[4,16384]{1,0:T(4,128)S(1)}, f32[4,16384]{1,0:T(4,128)}, u32[]{:S(2)}) copy-start(f32[4,16384]{1,0:T(4,128)} %refs_0_.1) | copy-start | bytes 786436
  14.3 8.9 %copy-start.3 = (f32[8,16384]{1,0:T(8,128)S(1)}, f32[8,16384]{1,0:T(8,128)}, u32[]{:S(2)}) copy-start(f32[8,16384]{1,0:T(8,128)} %refs_5_.4) | copy-start | bytes 1572868
  14.3 8.8 %copy-start.1 = (f32[8,16384]{1,0:T(8,128)S(1)}, f32[8,16384]{1,0:T(8,128)}, u32[]{:S(2)}) copy-start(f32[8,16384]{1,0:T(8,128)} %refs_4_.5) | copy-start | bytes 1572868
  14.4 7.0 %collective-permute-start.4 = (f32[4,4,4096]{2,1,0:T(4,128)S(1)}, f32[4,4,4096]{2,1,0:T(4,128)S(1)}, u32[]{:S(2)}, u32[]{:S(2)}) collective-permute-start(f32[4,4,4096]{2,1,0:T(4,128)S(1)} %pad_maximum_fusion.refs_0_), channel_id=1, source_target_pairs={{0,2},{1,3},{2,0},{3,1},{4,6},{5,7},{6,4},{7,5},{8,10},{9,11},{10,... | collective-permute-start | bytes 786440 | tf_op jit(solution)/shard_map/ppermute | solution.py:458
  16.0 5.7 %collective-permute-start.7 = (f32[3,4,4096]{2,1,0:T(4,128)S(1)}, f32[3,4,4096]{2,1,0:T(4,128)S(1)}, u32[]{:S(2)}, u32[]{:S(2)}) collective-permute-start(f32[3,4,4096]{2,1,0:T(4,128)S(1)} %pad_maximum_fusion.1), channel_id=1, source_target_pairs={{0,4},{4,0},{8,12},{12,8},{16,20},{20,16},{24,28},{28,24},{1,5},{5... | collective-permute-start | bytes 589832 | tf_op jit(solution)/shard_map/ppermute | solution.py:455
  16.6 6.5 %collective-permute-start.5 = (f32[4,4,4096]{2,1,0:T(4,128)S(1)}, f32[4,4,4096]{2,1,0:T(4,128)S(1)}, u32[]{:S(2)}, u32[]{:S(2)}) collective-permute-start(f32[4,4,4096]{2,1,0:T(4,128)S(1)} %pad_maximum_fusion.refs_0_), channel_id=1, source_target_pairs={{0,1},{1,0},{2,3},{3,2},{4,5},{5,4},{6,7},{7,6},{8,9},{9,8},{10,11... | collective-permute-start | bytes 786440 | tf_op jit(solution)/shard_map/ppermute | solution.py:458
  21.4 1.7 %collective-permute-start.6 = (f32[4,4,4096]{2,1,0:T(4,128)S(1)}, f32[4,4,4096]{2,1,0:T(4,128)S(1)}, u32[]{:S(2)}, u32[]{:S(2)}) collective-permute-start(f32[4,4,4096]{2,1,0:T(4,128)S(1)} %collective-permute-done.4.refs_1_), channel_id=1, source_target_pairs={{0,1},{1,0},{2,3},{3,2},{4,5},{5,4},{6,7},{7,6},{8,9},{9,8},{10,11... | collective-permute-start | bytes 786440 | tf_op jit(solution)/shard_map/ppermute | solution.py:458
  21.8 7.0 %collective-permute-start.8 = (f32[3,4,4096]{2,1,0:T(4,128)S(1)}, f32[3,4,4096]{2,1,0:T(4,128)S(1)}, u32[]{:S(2)}, u32[]{:S(2)}) collective-permute-start(f32[3,4,4096]{2,1,0:T(4,128)S(1)} %collective-permute-done.7.refs_0_), channel_id=1, source_target_pairs={{0,2},{1,3},{2,0},{3,1},{4,6},{5,7},{6,4},{7,5},{8,10},{9,11},{10,... | collective-permute-start | bytes 589832 | tf_op jit(solution)/shard_map/ppermute | solution.py:458
  22.9 5.8 %collective-permute-start.9 = (f32[3,4,4096]{2,1,0:T(4,128)S(1)}, f32[3,4,4096]{2,1,0:T(4,128)S(1)}, u32[]{:S(2)}, u32[]{:S(2)}) collective-permute-start(f32[3,4,4096]{2,1,0:T(4,128)S(1)} %collective-permute-done.7.refs_0_), channel_id=1, source_target_pairs={{0,1},{1,0},{2,3},{3,2},{4,5},{5,4},{6,7},{7,6},{8,9},{9,8},{10,11... | collective-permute-start | bytes 589832 | tf_op jit(solution)/shard_map/ppermute | solution.py:458
  28.7 4.5 %copy-start.6 = (bf16[768,128]{1,0:T(8,128)(2,1)S(1)}, bf16[768,128]{1,0:T(8,128)(2,1)}, u32[]{:S(2)}) copy-start(bf16[768,128]{1,0:T(8,128)(2,1)} %constant.38.refs_3_) | copy-start | bytes 589828
  28.7 1.4 %collective-permute-start.10 = (f32[3,4,4096]{2,1,0:T(4,128)S(1)}, f32[3,4,4096]{2,1,0:T(4,128)S(1)}, u32[]{:S(2)}, u32[]{:S(2)}) collective-permute-start(f32[3,4,4096]{2,1,0:T(4,128)S(1)} %shard_map.112.refs_1_), channel_id=1, source_target_pairs={{0,1},{1,0},{2,3},{3,2},{4,5},{5,4},{6,7},{7,6},{8,9},{9,8},{10,11... | collective-permute-start | bytes 589832 | tf_op jit(solution)/shard_map/ppermute | solution.py:458
  33.2 13.0 %copy-start.5 = (bf16[128,1536]{1,0:T(8,128)(2,1)S(1)}, bf16[128,1536]{1,0:T(8,128)(2,1)}, u32[]{:S(2)}) copy-start(bf16[128,1536]{1,0:T(8,128)(2,1)} %constant.43.refs_3_) | copy-start | bytes 1179652
  36.1 10.1 %copy-start.7 = (f32[256,128]{1,0:T(8,128)S(1)}, f32[256,128]{1,0:T(8,128)}, u32[]{:S(2)}) copy-start(f32[256,128]{1,0:T(8,128)} %constant.25.clone.refs_1_) | copy-start | bytes 393220
  36.1 10.1 %copy-start.8 = (f32[256,128]{1,0:T(8,128)S(1)}, f32[256,128]{1,0:T(8,128)}, u32[]{:S(2)}) copy-start(f32[256,128]{1,0:T(8,128)} %constant.26.clone.refs_2_) | copy-start | bytes 393220

commit v3 on v2

--- a/solution.py
+++ b/solution.py
@@ -12,7 +12,6 @@
 VMEM_BYTES = 16 * 1024 * 1024
 AXES = ("comp", "rank")
 PAD = 4
-HELD_PARTS = (0, 2, 1, 3)
 
 
 def split_parts(values):
@@ -235,29 +234,55 @@
     out, partial, joined, phases, weights, twiddle, table, arrivals = refs
     copies = start_tables(tables, (twiddle, table), arrivals)
     make_phases(groups, phases)
+    reduce_pieces(blocks, sources, pieces, columns, phases, weights, partial)
+    finish_pieces(
+        blocks, sources, copies, row_factors, twiddle, table, out, partial, joined
+    )
+
+
+def own_kernel(blocks, groups, sources, *refs):
+    row_factors, sent, refs = refs[0:2], refs[2:7], refs[7:]
+    out, partial, joined, phases, weights = refs[:5]
+    held, arrivals = refs[5:10], refs[10]
+    copies = start_tables(sent, held, arrivals)
+    make_phases(groups, phases)
+    for copy in copies[2:]:
+        copy.wait()
+    twiddle, table, own, *columns = held
+    reduce_pieces(blocks, sources, [own], columns, phases, weights, partial)
+    finish_pieces(
+        blocks, sources, copies[:2], row_factors, twiddle, table, out, partial, joined
+    )
+
+
+def reduce_pieces(blocks, sources, pieces, columns, phases, weights, partial):
     rows_here = pieces[0].shape[-2]
     terms, width = columns[0].shape
-    ranks = lax.axis_size("rank")
-    span = width // ranks
-    rank_at = lax.axis_index("rank")
-    starts = [(rank_at ^ other) * span for other in HELD_PARTS]
-    rows = len(sources) * rows_here
+    span = width // 2
+    core = lax.rem(lax.axis_index("rank"), 2)
+    starts = [core * span, (1 - core) * span]
 
     def fetch(part, row, lane):
-        quarters, index, _, _ = sources[row // rows_here]
+        halves, index, _, _ = sources[row // rows_here]
         row = pl.ds(row % rows_here, 1)
-        ref = pieces[quarters[part]]
+        ref = pieces[halves[part]]
         if index is None:
             return ref[row, pl.ds(pl.multiple_of(starts[part] + lane, LANES), LANES)]
         return ref[index, row, pl.ds(pl.multiple_of(lane, LANES), LANES)]
 
+    factors_at = made_factors(columns, phases, weights)
+    rows = len(sources) * rows_here
+    reduce_rows(blocks, rows, terms, fetch, factors_at, starts, span, partial)
+
+
+def finish_pieces(blocks, sources, copies, row_factors, twiddle, table, out, partial, joined):
+    rows = partial.shape[2]
+    rows_here = rows // len(sources)
     bases = [comp_of(step, flipped) * rows_here for _, _, step, flipped in sources]
 
     def row_at(row):
         return bases[row // rows_here] + row % rows_here
 
-    factors_at = made_factors(columns, phases, weights)
-    reduce_rows(blocks, rows, terms, fetch, factors_at, starts, span, partial)
     for copy in copies:
         copy.wait()
     transform_rows(blocks, rows, row_at, row_factors, twiddle, table, out, partial, joined)
@@ -294,19 +319,20 @@
     )
 
 
-def pass_kernel(value, earlier, out):
-    del value, earlier, out
-
-
-def after(value, earlier):
+def pass_kernel(*refs):
+    del refs
+
+
+def after(values, earlier):
     anywhere = pl.BlockSpec(memory_space=pl.ANY)
+    operands = [pltpu.with_memory_space_constraint(x, pltpu.VMEM) for x in (*values, earlier)]
     return pl.pallas_call(
         pass_kernel,
-        out_shape=jax.ShapeDtypeStruct(value.shape, value.dtype),
-        in_specs=[anywhere, anywhere],
-        out_specs=anywhere,
-        input_output_aliases={0: 0},
-    )(*[pltpu.with_memory_space_constraint(array, pltpu.VMEM) for array in (value, earlier)])
+        out_shape=[jax.ShapeDtypeStruct(value.shape, value.dtype) for value in values],
+        in_specs=[anywhere] * len(operands),
+        out_specs=[anywhere] * len(values),
+        input_output_aliases={k: k for k in range(len(values))},
+    )(*operands)
 
 
 def convolve_kernel(blocks, rows_here, layout, tile_count, *refs):
@@ -442,10 +468,11 @@
 def spectra_by_exchange(density, blocks, groups, columns, row_factors, tables):
     rows_here, width = density.shape
     comps, ranks = lax.axis_size("comp"), lax.axis_size("rank")
-    part = width // ranks
+    half = width // 2
     lines = comps // 2
     terms = row_factors[0].shape[0]
-    mine = lax.dynamic_slice_in_dim(density, lax.axis_index("rank") * part, part, 1)
+    core = lax.rem(lax.axis_index("rank"), 2)
+    mine = lax.dynamic_slice_in_dim(density, core * half, half, 1)
 
     def along(block, step):
         pairs = [(c, ((c // 2 + step) % lines) * 2 + c % 2) for c in range(comps)]
@@ -454,40 +481,41 @@
     def across(block):
         return lax.ppermute(block, "comp", [(c, c ^ 1) for c in range(comps)])
 
-    def swapped(block, other):
-        return lax.ppermute(block, "rank", [(r, r ^ other) for r in range(ranks)])
-
-    def spectra(pieces, sources):
+    def beside(block):
+        return lax.ppermute(block, "rank", [(r, r ^ 1) for r in range(ranks)])
+
+    def spectra(kernel, sources, operands, fetched):
         rows = rows_here * len(sources)
         (tile,) = whole_call(
-            lambda *refs: pieces_kernel(blocks, groups, sources, len(pieces), *refs),
+            lambda *refs: kernel(blocks, groups, sources, *refs),
             [(2 * blocks, 2, rows, terms, LANES)],
-            row_scratch(blocks, rows, terms, width, tables),
-            (*pieces, *columns, *row_factors),
-            tables,
+            row_scratch(blocks, rows, terms, width, fetched),
+            (*operands, *row_factors),
+            fetched,
         )
         return tile
 
+    def joined_spectra(pieces, sources):
+        def kernel(blocks, groups, sources, *refs):
+            pieces_kernel(blocks, groups, sources, len(pieces), *refs)
+
+        return spectra(kernel, sources, (*pieces, *columns), tables)
+
+    halves = (0, 1)
+    own_source = ((0, 0), None, 0, False)
+    early = [(halves, 0, 0, True)]
+    early += [(halves, step, step, False) for step in range(1, lines)]
+    late = [(halves, step - 1, step, True) for step in range(1, lines)]
+
     lined = [along(mine, step) for step in range(1, lines)]
-    own_source = ((0, 0, 0, 0), None, 0, False)
-    own = spectra([density], [own_source])
-    flipped_own = after(across(mine), own)
-    line_near = jnp.stack(lined)
-    near = jnp.concatenate([flipped_own[None], line_near])
-    flipped_near = across(line_near)
-    near_beyond = swapped(near, 2)
-    ready = [near, near_beyond, swapped(near, 1), swapped(near_beyond, 1)]
-    flipped_beyond = swapped(flipped_near, 2)
-    flipped_beside = swapped(flipped_near, 1)
-
-    quarters = (0, 1, 2, 3)
-    early = [(quarters, 0, 0, True)]
-    early += [(quarters, step, step, False) for step in range(1, lines)]
-    late = [(quarters, step - 1, step, True) for step in range(1, lines)]
-    first = spectra(ready, early)
-    flipped_beyond = after(flipped_beyond, first)
-    flipped = [flipped_near, flipped_beyond, flipped_beside, swapped(flipped_beyond, 1)]
-    second = spectra(flipped, late)
+    flipped_own = across(mine)
+    own = spectra(own_kernel, [own_source], (), (*tables, density, *columns))
+    (lined[lines // 2 - 1],) = after([lined[lines // 2 - 1]], own)
+    flipped = [across(block) for block in lined]
+    near = jnp.stack([flipped_own, *lined])
+    first = joined_spectra([near, beside(near)], early)
+    flipped_near = jnp.stack(after(flipped, first))
+    second = joined_spectra([flipped_near, beside(flipped_near)], late)
     layout = [source[2:] for source in [own_source] + early + late]
     return [own[None], first[None], second[None]], layout
 

time: 47.4 us -> 50.6 us (1.068)
  blocking collectives: 10.1 us -> 14.6 us
  local copies, waits for them, and re-layouts: 3.95 us -> 0.98 us
  Pallas kernels: 12.4 us -> 13.6 us
  waiting for transfers between devices: 8.4 us -> 9.51 us
  starting transfers between devices: 12 us -> 11.4 us
    ppermute x6 -> x2, waiting for transfers between devices: 8.05 us -> 1.71 us  [beside(): return lax.ppermute(block, 'rank', [(r, r ^ 1) for r in range(ranks)])]
    all_to_all x1, blocking collectives: 10.1 us -> 14.6 us  [body(): spread = lax.all_to_all(sent, AXES, split_axis=0, concat_axis=0, tiled=True)]
    ppermute x2 -> x4, waiting for transfers between devices: 0.35 us -> 4.09 us  [across(): return lax.ppermute(block, 'comp', [(c, c ^ 1) for c in range(comps)])]
    ppermute x3, waiting for transfers between devices: 0.01 us -> 3.71 us  [along(): return lax.ppermute(block, 'comp', pairs)]
    unnamed x22 -> x16, local copies, waits for them, and re-layouts: 3.08 us -> 0.04 us
    ppermute x6 -> x2, starting transfers between devices: 2.94 us -> 0.14 us  [beside(): return lax.ppermute(block, 'rank', [(r, r ^ 1) for r in range(ranks)])]
    ppermute x2 -> x4, starting transfers between devices: 3.54 us -> 5.16 us  [across(): return lax.ppermute(block, 'comp', [(c, c ^ 1) for c in range(comps)])]
    pallas_call x5, Pallas kernels: 12.4 us -> 13.6 us  [whole_call(): pl.pallas_call(kernel, out_shape=[out_type(shape, jnp.float32) for shape...]
  transfers between devices with their start and end apart: 11 -> 9, of which waited for: 4 -> 5; matrix products, arithmetic and copies ran while one was open for 0% -> 0% of each run, Pallas kernels for 12% -> 14%
where the time goes in v3:
time: 50.6 us; the launch traced here: 50.4 us
  blocking collectives  14.6 us (29%)
  Pallas kernels  13.6 us (27%)
  starting transfers between devices  11.4 us (23%)
  waiting for transfers between devices  9.51 us (19%)
  local copies, waits for them, and re-layouts  0.98 us (2%)
    all_to_all x1, blocking collectives, body(): spread = lax.all_to_all(sent, AXES, split_axis=0, concat_axis=0, tiled=True)  14.6 us
    pallas_call x5, Pallas kernels, whole_call(): pl.pallas_call(kernel, out_shape=[out_type(shape, jnp.float32) for shape...  13.6 us
    ppermute x3, starting transfers between devices, along(): return lax.ppermute(block, 'comp', pairs)  6.13 us
    ppermute x4, starting transfers between devices, across(): return lax.ppermute(block, 'comp', [(c, c ^ 1) for c in range(comps)])  5.16 us
    ppermute x4, waiting for transfers between devices, across(): return lax.ppermute(block, 'comp', [(c, c ^ 1) for c in range(comps)])  4.09 us
    ppermute x3, waiting for transfers between devices, along(): return lax.ppermute(block, 'comp', pairs)  3.71 us
    ppermute x2, waiting for transfers between devices, beside(): return lax.ppermute(block, 'rank', [(r, r ^ 1) for r in range(ranks)])  1.71 us
  transfers between devices with their start and end apart: 9, of which 5 were waited for; matrix products, arithmetic and copies ran while one was open for 0% of the time, Pallas kernels for 14%

profile of v3, /device:TPU:0, one launch (start us, length us, event | category | flops | bytes accessed | tf_op | source)
XLA Modules:
  0.0 50.4 jit_solution(10204533580802489987)
XLA Ops:
  0.0 0.0 copy-start.6
  0.0 0.0 copy-start.7
  0.0 0.9 %constant_dynamic-slice_fusion = f32[4,8192]{1,0:T(4,128)S(1)} fusion(f32[4,16384]{1,0:T(4,128)} %refs_4_.3, s32[]{:T(128)S(6)} %select_n.3), kind=kLoop, calls=%fused_computation.2 | loop fusion | bytes 262148 | tf_op jit(solution)/shard_map/dynamic_slice | solution.py:475
  0.9 4.1 %collective-permute-start.2 = (f32[4,8192]{1,0:T(4,128)S(1)}, f32[4,8192]{1,0:T(4,128)S(1)}, u32[]{:S(2)}, u32[]{:S(2)}) collective-permute-start(f32[4,8192]{1,0:T(4,128)S(1)} %constant_dynamic-slice_fusion), channel_id=1, source_target_pairs={{0,16},{4,20},{8,24},{12,28},{16,0},{20,4},{24,8},{28,12},{1,17},{... | collective-permute-start | bytes 393224 | tf_op jit(solution)/shard_map/ppermute | solution.py:479
  5.0 1.3 %collective-permute-start.3 = (f32[4,8192]{1,0:T(4,128)S(1)}, f32[4,8192]{1,0:T(4,128)S(1)}, u32[]{:S(2)}, u32[]{:S(2)}) collective-permute-start(f32[4,8192]{1,0:T(4,128)S(1)} %constant_dynamic-slice_fusion), channel_id=1, source_target_pairs={{0,24},{4,28},{8,0},{12,4},{16,8},{20,12},{24,16},{28,20},{1,25},{... | collective-permute-start | bytes 393224 | tf_op jit(solution)/shard_map/ppermute | solution.py:479
  6.4 0.7 %collective-permute-start.1 = (f32[4,8192]{1,0:T(4,128)S(1)}, f32[4,8192]{1,0:T(4,128)S(1)}, u32[]{:S(2)}, u32[]{:S(2)}) collective-permute-start(f32[4,8192]{1,0:T(4,128)S(1)} %constant_dynamic-slice_fusion), channel_id=1, source_target_pairs={{0,8},{4,12},{8,16},{12,20},{16,24},{20,28},{24,0},{28,4},{1,9},{5... | collective-permute-start | bytes 393224 | tf_op jit(solution)/shard_map/ppermute | solution.py:479
  7.1 1.5 %collective-permute-start = (f32[4,8192]{1,0:T(4,128)S(1)}, f32[4,8192]{1,0:T(4,128)S(1)}, u32[]{:S(2)}, u32[]{:S(2)}) collective-permute-start(f32[4,8192]{1,0:T(4,128)S(1)} %constant_dynamic-slice_fusion), channel_id=1, source_target_pairs={{0,4},{4,0},{8,12},{12,8},{16,20},{20,16},{24,28},{28,24},{1,5},{5... | collective-permute-start | bytes 393224 | tf_op jit(solution)/shard_map/ppermute | solution.py:482
  8.6 0.0 copy-done.6
  8.6 0.0 copy-done.7
  8.6 3.1 %shard_map.109.refs_1_ = f32[8,2,4,8,128]{4,3,2,1,0:T(8,128)S(1)} custom-call(f32[8,32]{1,0:T(8,128)S(1)} %copy-done.6, f32[8,32]{1,0:T(8,128)S(1)} %copy-done.7, f32[4,2,8,128]{3,2,1,0:T(8,128)} %constant.26.clone.refs_2_.refs_6_, bf16[768,256]{1,0:T(8,128)(2,1)} %constant.37.refs_3_.refs_7_, f32[4,16384]{1,0:T(4,128)} %refs_4_.3, f32[8,16384]{1,0:T(8,128)} %refs_2_.5, ...), custom_call_target="tpu_custom_call" | custom-call | tf_op jit(solution)/shard_map/pallas_call | solution.py:446
  11.7 1.3 %collective-permute-done.2.refs_0_ = f32[4,8192]{1,0:T(4,128)S(1)} collective-permute-done((f32[4,8192]{1,0:T(4,128)S(1)}, f32[4,8192]{1,0:T(4,128)S(1)}, u32[]{:S(2)}, u32[]{:S(2)}) %collective-permute-start.2) | collective-permute-done | bytes 131104 | tf_op jit(solution)/shard_map/ppermute | solution.py:479
  13.0 0.0 collective-permute-done.3
  13.0 2.4 %collective-permute-done.1 = f32[4,8192]{1,0:T(4,128)S(1)} collective-permute-done((f32[4,8192]{1,0:T(4,128)S(1)}, f32[4,8192]{1,0:T(4,128)S(1)}, u32[]{:S(2)}, u32[]{:S(2)}) %collective-permute-start.1) | collective-permute-done | bytes 131104 | tf_op jit(solution)/shard_map/ppermute | solution.py:479
  15.4 0.0 collective-permute-done
  15.4 0.0 copy-start
  15.4 0.0 copy-start.1
  15.4 0.1 pad_maximum_fusion.refs_0_
  15.5 0.1 collective-permute-start.4
  15.6 1.6 %collective-permute-start.7 = (f32[4,8192]{1,0:T(4,128)S(1)}, f32[4,8192]{1,0:T(4,128)S(1)}, u32[]{:S(2)}, u32[]{:S(2)}) collective-permute-start(f32[4,8192]{1,0:T(4,128)S(1)} %collective-permute-done.3), channel_id=1, source_target_pairs={{0,4},{4,0},{8,12},{12,8},{16,20},{20,16},{24,28},{28,24},{1,5},{5... | collective-permute-start | bytes 393224 | tf_op jit(solution)/shard_map/ppermute | solution.py:482
  17.2 0.5 %collective-permute-start.5 = (f32[4,8192]{1,0:T(4,128)S(1)}, f32[4,8192]{1,0:T(4,128)S(1)}, u32[]{:S(2)}, u32[]{:S(2)}) collective-permute-start(f32[4,8192]{1,0:T(4,128)S(1)} %collective-permute-done.1), channel_id=1, source_target_pairs={{0,4},{4,0},{8,12},{12,8},{16,20},{20,16},{24,28},{28,24},{1,5},{5... | collective-permute-start | bytes 393224 | tf_op jit(solution)/shard_map/ppermute | solution.py:482
  17.7 1.6 %collective-permute-start.6 = (f32[4,8192]{1,0:T(4,128)S(1)}, f32[4,8192]{1,0:T(4,128)S(1)}, u32[]{:S(2)}, u32[]{:S(2)}) collective-permute-start(f32[4,8192]{1,0:T(4,128)S(1)} %shard_map.110), channel_id=1, source_target_pairs={{0,4},{4,0},{8,12},{12,8},{16,20},{20,16},{24,28},{28,24},{1,5},{5... | collective-permute-start | bytes 393224 | tf_op jit(solution)/shard_map/ppermute | solution.py:482
  19.2 0.0 collective-permute-done.4.refs_1_
  19.2 0.0 copy-done
  19.2 0.0 copy-done.1
  19.2 3.8 %shard_map.111.refs_3_ = f32[8,2,16,8,128]{4,3,2,1,0:T(8,128)S(1)} custom-call(f32[4,4,8192]{2,1,0:T(4,128)S(1)} %pad_maximum_fusion.refs_0_, f32[4,4,8192]{2,1,0:T(4,128)S(1)} %collective-permute-done.4.refs_1_, f32[8,16384]{1,0:T(8,128)S(1)} %copy-done, f32[8,16384]{1,0:T(8,128)S(1)} %copy-done.1, f32[8,32]{1,0:T(8,128)S(1)} %copy-done.6, ...), custom_call_target="tpu_custom_call" | custom-call | tf_op jit(solution)/shard_map/pallas_call | solution.py:446
  23.0 0.0 collective-permute-done.7.refs_2_
  23.0 1.7 %collective-permute-done.5.refs_0_ = f32[4,8192]{1,0:T(4,128)S(1)} collective-permute-done((f32[4,8192]{1,0:T(4,128)S(1)}, f32[4,8192]{1,0:T(4,128)S(1)}, u32[]{:S(2)}, u32[]{:S(2)}) %collective-permute-start.5) | collective-permute-done | bytes 131104 | tf_op jit(solution)/shard_map/ppermute | solution.py:482
  24.8 2.4 %collective-permute-done.6.refs_1_ = f32[4,8192]{1,0:T(4,128)S(1)} collective-permute-done((f32[4,8192]{1,0:T(4,128)S(1)}, f32[4,8192]{1,0:T(4,128)S(1)}, u32[]{:S(2)}, u32[]{:S(2)}) %collective-permute-start.6) | collective-permute-done | bytes 131104 | tf_op jit(solution)/shard_map/ppermute | solution.py:482
  27.1 0.1 pad_maximum_fusion.1.refs_0_
  27.2 0.0 copy-start.3
  27.2 0.1 collective-permute-start.8
  27.3 1.7 %collective-permute-done.8.refs_1_ = f32[3,4,8192]{2,1,0:T(4,128)S(1)} collective-permute-done((f32[3,4,8192]{2,1,0:T(4,128)S(1)}, f32[3,4,8192]{2,1,0:T(4,128)S(1)}, u32[]{:S(2)}, u32[]{:S(2)}) %collective-permute-start.8) | collective-permute-done | bytes 393248 | tf_op jit(solution)/shard_map/ppermute | solution.py:485
  29.0 3.0 %shard_map.113 = f32[8,2,12,8,128]{4,3,2,1,0:T(8,128)S(1)} custom-call(f32[3,4,8192]{2,1,0:T(4,128)S(1)} %pad_maximum_fusion.1.refs_0_, f32[3,4,8192]{2,1,0:T(4,128)S(1)} %collective-permute-done.8.refs_1_, f32[8,16384]{1,0:T(8,128)S(1)} %copy-done, f32[8,16384]{1,0:T(8,128)S(1)} %copy-done.1, f32[8,32]{1,0:T(8,128)S(1)} %copy-done.6, ...), custom_call_target="tpu_custom_call" | custom-call | tf_op jit(solution)/shard_map/pallas_call | solution.py:446
  32.1 0.0 copy-done.3
  32.1 0.0 copy-start.2
  32.1 2.9 %shard_map.114 = f32[256,128]{1,0:T(8,128)S(1)} custom-call(f32[1,8,2,4,8,128]{5,4,3,2,1,0:T(8,128)S(1)} %bitcast.15, f32[1,8,2,16,8,128]{5,4,3,2,1,0:T(8,128)S(1)} %bitcast.13, f32[1,8,2,12,8,128]{5,4,3,2,1,0:T(8,128)S(1)} %bitcast.14, bf16[768,128]{1,0:T(8,128)(2,1)S(1)} %copy-done.3), custom_call_target="tpu_custom_call" | custom-call | tf_op jit(solution)/shard_map/pallas_call | solution.py:446
  35.0 0.0 copy-start.4
  35.0 0.0 copy-start.5
  35.0 14.6 %all_to_all.11 = f32[32,8,128]{2,1,0:T(8,128)S(1)} all-to-all(f32[32,8,128]{2,1,0:T(8,128)S(1)} %bitcast.16), channel_id=1, replica_groups=mesh['comp'=8,'rank'=4] {'comp','rank'}, dimensions={0} | all-to-all | bytes 262144 | tf_op jit(solution)/shard_map/all_to_all | solution.py:578
  49.5 0.0 copy-done.2
  49.5 0.0 copy-done.4
  49.5 0.0 copy-done.5
  49.6 0.9 %shard_map.115 = f32[128,128]{1,0:T(8,128)} custom-call(f32[256,128]{1,0:T(8,128)S(1)} %bitcast.17, f32[256,128]{1,0:T(8,128)S(1)} %copy-done.5, f32[256,128]{1,0:T(8,128)S(1)} %copy-done.4, bf16[128,1536]{1,0:T(8,128)(2,1)S(1)} %copy-done.2), custom_call_target="tpu_custom_call" | custom-call | tf_op jit(solution)/shard_map/pallas_call | solution.py:446
  (2 shorter events, 0.0 us)
Async XLA Ops:
  0.0 8.6 %copy-start.6 = (f32[8,32]{1,0:T(8,128)S(1)}, f32[8,32]{1,0:T(8,128)}, u32[]{:S(2)}) copy-start(f32[8,32]{1,0:T(8,128)} %refs_4_.5) | copy-start | bytes 3076
  0.0 8.6 %copy-start.7 = (f32[8,32]{1,0:T(8,128)S(1)}, f32[8,32]{1,0:T(8,128)}, u32[]{:S(2)}) copy-start(f32[8,32]{1,0:T(8,128)} %refs_5_.5) | copy-start | bytes 3076
  0.9 12.1 %collective-permute-start.2 = (f32[4,8192]{1,0:T(4,128)S(1)}, f32[4,8192]{1,0:T(4,128)S(1)}, u32[]{:S(2)}, u32[]{:S(2)}) collective-permute-start(f32[4,8192]{1,0:T(4,128)S(1)} %constant_dynamic-slice_fusion), channel_id=1, source_target_pairs={{0,16},{4,20},{8,24},{12,28},{16,0},{20,4},{24,8},{28,12},{1,17},{... | collective-permute-start | bytes 393224 | tf_op jit(solution)/shard_map/ppermute | solution.py:479
  5.0 8.0 %collective-permute-start.3 = (f32[4,8192]{1,0:T(4,128)S(1)}, f32[4,8192]{1,0:T(4,128)S(1)}, u32[]{:S(2)}, u32[]{:S(2)}) collective-permute-start(f32[4,8192]{1,0:T(4,128)S(1)} %constant_dynamic-slice_fusion), channel_id=1, source_target_pairs={{0,24},{4,28},{8,0},{12,4},{16,8},{20,12},{24,16},{28,20},{1,25},{... | collective-permute-start | bytes 393224 | tf_op jit(solution)/shard_map/ppermute | solution.py:479
  6.4 9.0 %collective-permute-start.1 = (f32[4,8192]{1,0:T(4,128)S(1)}, f32[4,8192]{1,0:T(4,128)S(1)}, u32[]{:S(2)}, u32[]{:S(2)}) collective-permute-start(f32[4,8192]{1,0:T(4,128)S(1)} %constant_dynamic-slice_fusion), channel_id=1, source_target_pairs={{0,8},{4,12},{8,16},{12,20},{16,24},{20,28},{24,0},{28,4},{1,9},{5... | collective-permute-start | bytes 393224 | tf_op jit(solution)/shard_map/ppermute | solution.py:479
  7.1 8.3 %collective-permute-start = (f32[4,8192]{1,0:T(4,128)S(1)}, f32[4,8192]{1,0:T(4,128)S(1)}, u32[]{:S(2)}, u32[]{:S(2)}) collective-permute-start(f32[4,8192]{1,0:T(4,128)S(1)} %constant_dynamic-slice_fusion), channel_id=1, source_target_pairs={{0,4},{4,0},{8,12},{12,8},{16,20},{20,16},{24,28},{28,24},{1,5},{5... | collective-permute-start | bytes 393224 | tf_op jit(solution)/shard_map/ppermute | solution.py:482
  15.4 3.9 %copy-start = (f32[8,16384]{1,0:T(8,128)S(1)}, f32[8,16384]{1,0:T(8,128)}, u32[]{:S(2)}) copy-start(f32[8,16384]{1,0:T(8,128)} %refs_2_.5) | copy-start | bytes 1572868
  15.4 3.9 %copy-start.1 = (f32[8,16384]{1,0:T(8,128)S(1)}, f32[8,16384]{1,0:T(8,128)}, u32[]{:S(2)}) copy-start(f32[8,16384]{1,0:T(8,128)} %refs_3_.3) | copy-start | bytes 1572868
  15.5 3.7 %collective-permute-start.4 = (f32[4,4,8192]{2,1,0:T(4,128)S(1)}, f32[4,4,8192]{2,1,0:T(4,128)S(1)}, u32[]{:S(2)}, u32[]{:S(2)}) collective-permute-start(f32[4,4,8192]{2,1,0:T(4,128)S(1)} %pad_maximum_fusion.refs_0_), channel_id=1, source_target_pairs={{0,1},{1,0},{2,3},{3,2},{4,5},{5,4},{6,7},{7,6},{8,9},{9,8},{10,11... | collective-permute-start | bytes 1572872 | tf_op jit(solution)/shard_map/ppermute | solution.py:485
  15.6 7.4 %collective-permute-start.7 = (f32[4,8192]{1,0:T(4,128)S(1)}, f32[4,8192]{1,0:T(4,128)S(1)}, u32[]{:S(2)}, u32[]{:S(2)}) collective-permute-start(f32[4,8192]{1,0:T(4,128)S(1)} %collective-permute-done.3), channel_id=1, source_target_pairs={{0,4},{4,0},{8,12},{12,8},{16,20},{20,16},{24,28},{28,24},{1,5},{5... | collective-permute-start | bytes 393224 | tf_op jit(solution)/shard_map/ppermute | solution.py:482
  17.2 7.6 %collective-permute-start.5 = (f32[4,8192]{1,0:T(4,128)S(1)}, f32[4,8192]{1,0:T(4,128)S(1)}, u32[]{:S(2)}, u32[]{:S(2)}) collective-permute-start(f32[4,8192]{1,0:T(4,128)S(1)} %collective-permute-done.1), channel_id=1, source_target_pairs={{0,4},{4,0},{8,12},{12,8},{16,20},{20,16},{24,28},{28,24},{1,5},{5... | collective-permute-start | bytes 393224 | tf_op jit(solution)/shard_map/ppermute | solution.py:482
  17.7 9.4 %collective-permute-start.6 = (f32[4,8192]{1,0:T(4,128)S(1)}, f32[4,8192]{1,0:T(4,128)S(1)}, u32[]{:S(2)}, u32[]{:S(2)}) collective-permute-start(f32[4,8192]{1,0:T(4,128)S(1)} %shard_map.110), channel_id=1, source_target_pairs={{0,4},{4,0},{8,12},{12,8},{16,20},{20,16},{24,28},{28,24},{1,5},{5... | collective-permute-start | bytes 393224 | tf_op jit(solution)/shard_map/ppermute | solution.py:482
  27.2 4.8 %copy-start.3 = (bf16[768,128]{1,0:T(8,128)(2,1)S(1)}, bf16[768,128]{1,0:T(8,128)(2,1)}, u32[]{:S(2)}) copy-start(bf16[768,128]{1,0:T(8,128)(2,1)} %constant.42.refs_3_) | copy-start | bytes 589828
  27.2 1.8 %collective-permute-start.8 = (f32[3,4,8192]{2,1,0:T(4,128)S(1)}, f32[3,4,8192]{2,1,0:T(4,128)S(1)}, u32[]{:S(2)}, u32[]{:S(2)}) collective-permute-start(f32[3,4,8192]{2,1,0:T(4,128)S(1)} %pad_maximum_fusion.1.refs_0_), channel_id=1, source_target_pairs={{0,1},{1,0},{2,3},{3,2},{4,5},{5,4},{6,7},{7,6},{8,9},{9,8},{10,11... | collective-permute-start | bytes 1179656 | tf_op jit(solution)/shard_map/ppermute | solution.py:485
  32.1 17.5 %copy-start.2 = (bf16[128,1536]{1,0:T(8,128)(2,1)S(1)}, bf16[128,1536]{1,0:T(8,128)(2,1)}, u32[]{:S(2)}) copy-start(bf16[128,1536]{1,0:T(8,128)(2,1)} %constant.47.refs_3_) | copy-start | bytes 1179652
  35.0 14.6 %copy-start.4 = (f32[256,128]{1,0:T(8,128)S(1)}, f32[256,128]{1,0:T(8,128)}, u32[]{:S(2)}) copy-start(f32[256,128]{1,0:T(8,128)} %constant.30.clone.refs_2_) | copy-start | bytes 393220
  35.0 14.6 %copy-start.5 = (f32[256,128]{1,0:T(8,128)S(1)}, f32[256,128]{1,0:T(8,128)}, u32[]{:S(2)}) copy-start(f32[256,128]{1,0:T(8,128)} %constant.29.clone.refs_1_) | copy-start | bytes 393220
